TPU v7x, 32 devices: a whole 2x2x4 slice. The times are simulated.
32 devices in a mesh: gx: 2 (over x), gy: 4 (over z), ga: 4 (over y, core).
Axes of the slice: x: 2, y: 2, z: 4, core: 2. Of those that a mesh axis runs over, the one named last changes fastest.
Arguments:
- fixed: float32 [16, 32, 512], P('gx', 'gy', 'ga'), may hold values from -6 to 6
- moving: float32 [16, 32, 512], P('gx', 'gy', 'ga'), may hold values from -6 to 6
- coarse_disp: float32 [3, 4, 8, 128], P(None, 'gx', 'gy', 'ga'), may hold values from -6 to 6
- offsets: int32 [3, 4, 8, 128], P(None, 'gx', 'gy', 'ga'), may hold values from -2 to 1
Outputs:
- similarity: float32 [], replicated
- grad_coarse: float32 [3, 4, 8, 128], P(None, 'gx', 'gy', 'ga')
All inputs are finite; a program needn't handle non-finite values.
Results may differ from a plain program's by a relative error of at most 0.0003.
Values sent between devices are 32-bit elements; how exact they have to be, the bound alone decides.
A program may use at most 64 MiB of HBM per device.

v0:
```python
import jax
import jax.numpy as jnp
from jax import lax
from jax.sharding import PartitionSpec as P

window_count = 729.0
epsilon = 1e-05


def extended(cells, sides, width):
    for axis, dim in sides:
        count = lax.axis_size(axis)
        ends = count - 1
        head = lax.slice_in_dim(cells, 0, width, axis=dim)
        tail = lax.slice_in_dim(cells, cells.shape[dim] - width, cells.shape[dim], axis=dim)
        cells = jnp.concatenate(
            [
                lax.ppermute(tail, axis, [(i, (i + 1) % count) for i in range(ends)]),
                cells,
                lax.ppermute(head, axis, [((i + 1) % count, i) for i in range(ends)]),
            ],
            axis=dim,
        )
    return cells


def smooth_padded(padded):
    padded = (padded[:, :-2] + 2.0 * padded[:, 1:-1] + padded[:, 2:]) * 0.25
    padded = (padded[:, :, :-2] + 2.0 * padded[:, :, 1:-1] + padded[:, :, 2:]) * 0.25
    return (padded[:, :, :, :-2] + 2.0 * padded[:, :, :, 1:-1] + padded[:, :, :, 2:]) * 0.25


def upsample(coarse):
    return jnp.repeat(jnp.repeat(jnp.repeat(coarse, 4, axis=1), 4, axis=2), 4, axis=3)


def shift_weights(fine_offsets, fractions, axis_number):
    offset_k = fine_offsets[axis_number]
    frac_k = fractions[axis_number]
    weights = []
    for shift in range(-2, 3):
        lower = (offset_k == shift).astype(frac_k.dtype)
        upper = (offset_k + 1 == shift).astype(frac_k.dtype)
        weights.append((lower * (1.0 - frac_k) + upper * frac_k, upper - lower))
    return weights


def warp(moving_pad, fine_offsets, fractions):
    size_x, size_y, size_z = fine_offsets.shape[1:]
    weights_x = shift_weights(fine_offsets, fractions, 0)
    weights_y = shift_weights(fine_offsets, fractions, 1)
    weights_z = shift_weights(fine_offsets, fractions, 2)
    warped = None
    for index_x in range(5):
        wx, dx = weights_x[index_x]
        mid_w = None
        for index_y in range(5):
            wy, dy = weights_y[index_y]
            inner_w = None
            for index_z in range(5):
                wz, dz = weights_z[index_z]
                values = lax.slice(
                    moving_pad,
                    (index_x, index_y, index_z),
                    (index_x + size_x, index_y + size_y, index_z + size_z),
                )
                if inner_w is None:
                    inner_w = wz * values
                    inner_d = dz * values
                else:
                    inner_w = inner_w + wz * values
                    inner_d = inner_d + dz * values
            if mid_w is None:
                mid_w = wy * inner_w
                mid_dy = dy * inner_w
                mid_dz = wy * inner_d
            else:
                mid_w = mid_w + wy * inner_w
                mid_dy = mid_dy + dy * inner_w
                mid_dz = mid_dz + wy * inner_d
        if warped is None:
            warped = wx * mid_w
            slope_x = dx * mid_w
            slope_y = wx * mid_dy
            slope_z = wx * mid_dz
        else:
            warped = warped + wx * mid_w
            slope_x = slope_x + dx * mid_w
            slope_y = slope_y + wx * mid_dy
            slope_z = slope_z + wx * mid_dz
    return (warped, jnp.stack([slope_x, slope_y, slope_z]))


def box_axis(values, axis):
    length = values.shape[axis] - 8
    total = lax.slice_in_dim(values, 0, length, axis=axis)
    for start in range(1, 9):
        total = total + lax.slice_in_dim(values, start, start + length, axis=axis)
    return total


def box_sum(values):
    values = box_axis(values, values.ndim - 3)
    values = box_axis(values, values.ndim - 2)
    return box_axis(values, values.ndim - 1)


def lncc(fixed_ext, warped_ext):
    fields = jnp.stack(
        [
            fixed_ext,
            warped_ext,
            fixed_ext * fixed_ext,
            warped_ext * warped_ext,
            fixed_ext * warped_ext,
        ]
    )
    sums = box_sum(fields)
    fixed_sum, warped_sum = (sums[0], sums[1])
    cross = sums[4] - fixed_sum * warped_sum / window_count
    fixed_var = sums[2] - fixed_sum * fixed_sum / window_count
    warped_var = sums[3] - warped_sum * warped_sum / window_count
    denom = fixed_var * warped_var + epsilon
    similar = cross * cross / denom
    coef_a = 2.0 * cross / denom
    coef_b = -cross * cross * fixed_var / (denom * denom)
    coef_c = -(coef_a * fixed_sum + 2.0 * coef_b * warped_sum) / window_count
    return (similar, jnp.stack([coef_a, coef_b, coef_c]))


def restrict_grad(grad_warped, slopes, smoothed):
    grad_frac = grad_warped[None] * slopes
    chans, size_x, size_y, size_z = grad_frac.shape
    restricted = grad_frac.reshape(chans, size_x // 4, 4, size_y // 4, 4, size_z // 4, 4).sum(
        axis=(2, 4, 6)
    )
    sigmoid_value = jax.nn.sigmoid(smoothed)
    return restricted * sigmoid_value * (1.0 - sigmoid_value)


def on_device(fixed, moving, coarse_disp, offsets):
    size_x, size_y, size_z = fixed.shape
    coarse_pad = extended(coarse_disp, (("gx", 1), ("gy", 2), ("ga", 3)), 1)
    smoothed = smooth_padded(coarse_pad)
    fractions = upsample(jax.nn.sigmoid(smoothed))
    fine_offsets = upsample(offsets)
    moving_pad = extended(moving, (("gx", 0), ("gy", 1), ("ga", 2)), 2)
    warped, slopes = warp(moving_pad, fine_offsets, fractions)
    images = extended(jnp.stack([fixed, warped]), (("gx", 1), ("gy", 2), ("ga", 3)), 4)
    fixed_ext = images[0]
    warped_ext = images[1]
    similar, coeffs = lncc(fixed_ext, warped_ext)
    total = lax.psum(jnp.sum(similar), ("gx", "gy", "ga"))
    voxel_count = (
        size_x * size_y * size_z * lax.axis_size("gx") * lax.axis_size("gy") * lax.axis_size("ga")
    )
    similarity = total / jnp.float32(voxel_count)
    coeff_ext = extended(coeffs, (("gx", 1), ("gy", 2), ("ga", 3)), 4)
    boxed = box_sum(coeff_ext)
    grad_warped = -(fixed * boxed[0] + 2.0 * warped * boxed[1] + boxed[2])
    grad_smooth = restrict_grad(grad_warped, slopes, smoothed)
    grad_pad = extended(grad_smooth, (("gx", 1), ("gy", 2), ("ga", 3)), 1)
    grad_coarse = smooth_padded(grad_pad)
    return (similarity, grad_coarse)


def solution(mesh):
    in_specs = (
        P("gx", "gy", "ga"),
        P("gx", "gy", "ga"),
        P(None, "gx", "gy", "ga"),
        P(None, "gx", "gy", "ga"),
    )
    out_specs = (P(), P(None, "gx", "gy", "ga"))
    return jax.shard_map(
        on_device, mesh=mesh, in_specs=in_specs, out_specs=out_specs, check_vma=False
    )
```

profile of v0, /device:TPU:0, one launch (start us, length us, event | category | flops | bytes accessed | tf_op | source)
XLA Modules:
  0.0 221.1 jit_solution(9589488193033223935)
XLA Ops:
  1.3 4.8 %collective-permute-start = (f32[3,1,2,32]{3,2,1,0:T(2,128)S(1)}, f32[3,1,2,32]{3,2,1,0:T(2,128)S(1)}, u32[]{:S(2)}, u32[]{:S(2)}) collective-permute-start(f32[3,1,2,32]{3,2,1,0:T(2,128)S(1)} %get-tuple-element.127), channel_id=1, source_target_pairs={{0,16},{1,17},{2,18},{3,19},{4,20},{5,21},{6,22},{7,23},{8,24},{9,... | collective-permute-start | bytes 2312 | tf_op jit(solution)/shard_map/ppermute | solution.py:18
  8.8 5.1 %collective-permute-start.6 = (f32[2,8,128]{2,1,0:T(8,128)}, f32[2,8,128]{2,1,0:T(8,128)}, u32[]{:S(2)}, u32[]{:S(2)}) collective-permute-start(f32[2,8,128]{2,1,0:T(8,128)} %get-tuple-element.78), channel_id=1, source_target_pairs={{0,16},{1,17},{2,18},{3,19},{4,20},{5,21},{6,22},{7,23},{8,24},{9,... | collective-permute-start | bytes 24584 | tf_op jit(solution)/shard_map/ppermute | solution.py:18
  30.8 3.5 %collective-permute-start.2 = (f32[3,4,1,32]{3,2,1,0:T(1,128)S(1)}, f32[3,4,1,32]{3,2,1,0:T(1,128)S(1)}, u32[]{:S(2)}, u32[]{:S(2)}) collective-permute-start(f32[3,4,1,32]{3,2,1,0:T(1,128)S(1)} %get-tuple-element.85), channel_id=1, source_target_pairs={{0,4},{4,8},{8,12},{1,5},{5,9},{9,13},{2,6},{6,10},{10,14},{3,7},{... | collective-permute-start | bytes 4616 | tf_op jit(solution)/shard_map/ppermute | solution.py:18
  46.7 2.8 %collective-permute-done.5 = f32[3,4,4,1]{3,2,1,0:T(4,128)S(1)} collective-permute-done((f32[3,4,4,1]{3,2,1,0:T(4,128)S(1)}, f32[3,4,4,1]{3,2,1,0:T(4,128)S(1)}, u32[]{:S(2)}, u32[]{:S(2)}) %collective-permute-start.5) | collective-permute-done | bytes 224 | tf_op jit(solution)/shard_map/ppermute | solution.py:20
  56.5 5.1 %collective-permute-start.8 = (f32[12,2,128]{2,1,0:T(2,128)}, f32[12,2,128]{2,1,0:T(2,128)}, u32[]{:S(2)}, u32[]{:S(2)}) collective-permute-start(f32[12,2,128]{2,1,0:T(2,128)} %get-tuple-element.72), channel_id=1, source_target_pairs={{0,4},{4,8},{8,12},{1,5},{5,9},{9,13},{2,6},{6,10},{10,14},{3,7},{... | collective-permute-start | bytes 36872 | tf_op jit(solution)/shard_map/ppermute | solution.py:18
  62.9 2.5 %select_add_fusion.14 = (f32[8,8,32,4]{1,0,3,2:T(8,128)}, f32[8,8,32,4]{1,0,3,2:T(8,128)}, f32[8,8,32,4]{1,0,3,2:T(8,128)}, f32[8,8,32,4]{1,0,3,2:T(8,128)}, f32[8,8,32,4]{1,0,3,2:T(8,128)}) fusion(f32[8,8,32]{1,0,2:T(8,128)S(1)} %copy.617, f32[8,8,32]{1,0,2:T(8,128)S(1)} %copy.614, pred[8,8,32]{1,0,2:T(8,128)(4,1)} %copy.616, pred[8,8,32]{1,0,2:T(8,128)(4,1)} %copy.612, ...), kind=kLoop, calls=%fused_computation.25 | loop fusion | flops 122880 | bytes 200704 | tf_op jit(solution)/shard_map/add | solution.py:44
  68.4 1.8 copy.632
  72.6 4.8 %collective-permute-start.10 = (f32[12,12,2]{2,1,0:T(8,128)}, f32[12,12,2]{2,1,0:T(8,128)}, u32[]{:S(2)}, u32[]{:S(2)}) collective-permute-start(f32[12,12,2]{2,1,0:T(8,128)} %get-tuple-element.66), channel_id=1, source_target_pairs={{0,1},{1,2},{2,3},{4,5},{5,6},{6,7},{8,9},{9,10},{10,11},{12,13},{... | collective-permute-start | bytes 3464 | tf_op jit(solution)/shard_map/ppermute | solution.py:18
  83.6 2.9 %multiply_add_fusion.2 = (f32[8,8,128]{2,1,0:T(8,128)}, f32[8,8,128]{2,1,0:T(8,128)S(1)}, f32[8,8,128]{2,1,0:T(8,128)S(1)}, f32[8,8,128]{2,1,0:T(8,128)S(1)}, f3...) fusion(f32[8,8,128]{2,1,0:T(8,128)S(1)} %copy-done.11, ...), kind=kLoop, calls=%fused_computation.167 | loop fusion | flops 2449408 | bytes 5021696 | tf_op jit(solution)/shard_map/add | solution.py:88
  86.5 5.1 %collective-permute-start.12 = (f32[2,4,8,128]{3,2,1,0:T(8,128)S(1)}, f32[2,4,8,128]{3,2,1,0:T(8,128)S(1)}, u32[]{:S(2)}, u32[]{:S(2)}) collective-permute-start(f32[2,4,8,128]{3,2,1,0:T(8,128)S(1)} %get-tuple-element.70), channel_id=1, source_target_pairs={{0,16},{1,17},{2,18},{3,19},{4,20},{5,21},{6,22},{7,23},{8,24},{9,... | collective-permute-start | bytes 98312 | tf_op jit(solution)/shard_map/ppermute | solution.py:18
  93.3 4.4 %collective-permute-done.13 = f32[2,4,8,128]{3,2,1,0:T(8,128)S(1)} collective-permute-done((f32[2,4,8,128]{3,2,1,0:T(8,128)S(1)}, f32[2,4,8,128]{3,2,1,0:T(8,128)S(1)}, u32[]{:S(2)}, u32[]{:S(2)}) %collective-permute-start.13) | collective-permute-done | bytes 32800 | tf_op jit(solution)/shard_map/ppermute | solution.py:20
  97.8 4.3 %collective-permute-start.14 = (f32[2,16,4,128]{3,1,2,0:T(8,128)S(1)}, f32[2,16,4,128]{3,1,2,0:T(8,128)S(1)}, u32[]{:S(2)}, u32[]{:S(2)}) collective-permute-start(f32[2,16,4,128]{3,1,2,0:T(8,128)S(1)} %copy.1052), channel_id=1, source_target_pairs={{0,4},{4,8},{8,12},{1,5},{5,9},{9,13},{2,6},{6,10},{10,14},{3,7},{... | collective-permute-start | bytes 196616 | tf_op jit(solution)/shard_map/ppermute | solution.py:18
  104.0 4.3 %collective-permute-done.15 = f32[2,16,4,128]{3,1,2,0:T(8,128)S(1)} collective-permute-done((f32[2,16,4,128]{3,1,2,0:T(8,128)S(1)}, f32[2,16,4,128]{3,1,2,0:T(8,128)S(1)}, u32[]{:S(2)}, u32[]{:S(2)}) %collective-permute-start.15) | collective-permute-done | bytes 65568 | tf_op jit(solution)/shard_map/ppermute | solution.py:20
  111.3 4.1 %collective-permute-done.17 = f32[2,16,16,4]{3,2,1,0:T(8,128)S(1)} collective-permute-done((f32[2,16,16,4]{3,2,1,0:T(8,128)S(1)}, f32[2,16,16,4]{3,2,1,0:T(8,128)S(1)}, u32[]{:S(2)}, u32[]{:S(2)}) %collective-permute-start.17) | collective-permute-done | bytes 8224 | tf_op jit(solution)/shard_map/ppermute | solution.py:20
  118.0 1.6 collective-permute-start.18
  128.1 3.0 %collective-permute-start.20 = (f32[3,16,4,128]{3,1,2,0:T(8,128)S(1)}, f32[3,16,4,128]{3,1,2,0:T(8,128)S(1)}, u32[]{:S(2)}, u32[]{:S(2)}) collective-permute-start(f32[3,16,4,128]{3,1,2,0:T(8,128)S(1)} %copy.1054), channel_id=1, source_target_pairs={{0,4},{4,8},{8,12},{1,5},{5,9},{9,13},{2,6},{6,10},{10,14},{3,7},{... | collective-permute-start | bytes 294920 | tf_op jit(solution)/shard_map/ppermute | solution.py:18
  132.5 2.7 %multiply_add_fusion = f32[8,8,128]{2,1,0:T(8,128)} fusion(f32[8,8,128]{2,1,0:T(8,128)S(1)} %copy.834, f32[8,8,128]{2,1,0:T(8,128)S(1)} %copy.693, f32[8,8,128]{2,1,0:T(8,128)S(1)} %copy.898, f32[8,8,128]{2,1,0:T(8,128)S(1)} %copy.896, f32[8,8,128]{2,1,0:T(8,128)S(1)} %copy.894, f32[8,8,128]{2,1,0:T(8,128)S(1)} %copy.892, f32[8,8,128]{2,1,0:T(8,128)S(1)} %copy.890, ...), kind=kLoop, calls=%fused_computation.155 | loop fusion | flops 2449408 | bytes 4038656 | tf_op jit(solution)/shard_map/add | solution.py:90
  135.4 2.3 %collective-permute-done.21 = f32[3,16,4,128]{3,1,2,0:T(8,128)S(1)} collective-permute-done((f32[3,16,4,128]{3,1,2,0:T(8,128)S(1)}, f32[3,16,4,128]{3,1,2,0:T(8,128)S(1)}, u32[]{:S(2)}, u32[]{:S(2)}) %collective-permute-start.21) | collective-permute-done | bytes 98336 | tf_op jit(solution)/shard_map/ppermute | solution.py:20
  138.0 5.3 %collective-permute-start.22 = (f32[3,16,16,4]{3,2,1,0:T(8,128)S(1)}, f32[3,16,16,4]{3,2,1,0:T(8,128)S(1)}, u32[]{:S(2)}, u32[]{:S(2)}) collective-permute-start(f32[3,16,16,4]{3,2,1,0:T(8,128)S(1)} %get-tuple-element.41), channel_id=1, source_target_pairs={{0,1},{1,2},{2,3},{4,5},{5,6},{6,7},{8,9},{9,10},{10,11},{12,13},{... | collective-permute-start | bytes 36872 | tf_op jit(solution)/shard_map/ppermute | solution.py:18
  153.5 4.3 %collective-permute-start.24 = (f32[3,1,2,32]{3,2,1,0:T(2,128)S(1)}, f32[3,1,2,32]{3,2,1,0:T(2,128)S(1)}, u32[]{:S(2)}, u32[]{:S(2)}) collective-permute-start(f32[3,1,2,32]{3,2,1,0:T(2,128)S(1)} %get-tuple-element.91), channel_id=1, source_target_pairs={{0,16},{1,17},{2,18},{3,19},{4,20},{5,21},{6,22},{7,23},{8,24},{9,... | collective-permute-start | bytes 2312 | tf_op jit(solution)/shard_map/ppermute | solution.py:18
  159.1 4.2 %collective-permute-done.25 = f32[3,1,2,32]{3,2,1,0:T(2,128)S(1)} collective-permute-done((f32[3,1,2,32]{3,2,1,0:T(2,128)S(1)}, f32[3,1,2,32]{3,2,1,0:T(2,128)S(1)}, u32[]{:S(2)}, u32[]{:S(2)}) %collective-permute-start.25) | collective-permute-done | bytes 800 | tf_op jit(solution)/shard_map/ppermute | solution.py:20
  163.3 3.6 %collective-permute-start.26 = (f32[3,4,1,32]{3,2,1,0:T(1,128)S(1)}, f32[3,4,1,32]{3,2,1,0:T(1,128)S(1)}, u32[]{:S(2)}, u32[]{:S(2)}) collective-permute-start(f32[3,4,1,32]{3,2,1,0:T(1,128)S(1)} %get-tuple-element.83), channel_id=1, source_target_pairs={{0,4},{4,8},{8,12},{1,5},{5,9},{9,13},{2,6},{6,10},{10,14},{3,7},{... | collective-permute-start | bytes 4616 | tf_op jit(solution)/shard_map/ppermute | solution.py:18
  168.9 43.0 %psum.7 = f32[]{:T(128)} all-reduce(f32[]{:T(128)} %fusion.29), channel_id=1, replica_groups=mesh['gx'=2,'gy'=4,'ga'=4] {'gx','gy','ga'}, use_global_device_ids=true, to_apply=%region_1.0 | all-reduce | flops 1 | bytes 8 | tf_op jit(solution)/shard_map/psum | solution.py:153
  215.3 3.8 %collective-permute-done.29 = f32[3,4,4,1]{3,2,1,0:T(4,128)S(1)} collective-permute-done((f32[3,4,4,1]{3,2,1,0:T(4,128)S(1)}, f32[3,4,4,1]{3,2,1,0:T(4,128)S(1)}, u32[]{:S(2)}, u32[]{:S(2)}) %collective-permute-start.29) | collective-permute-done | bytes 224 | tf_op jit(solution)/shard_map/ppermute | solution.py:20
  (500 shorter events, 86.5 us)
Async XLA Ops:
  1.3 29.4 %collective-permute-start = (f32[3,1,2,32]{3,2,1,0:T(2,128)S(1)}, f32[3,1,2,32]{3,2,1,0:T(2,128)S(1)}, u32[]{:S(2)}, u32[]{:S(2)}) collective-permute-start(f32[3,1,2,32]{3,2,1,0:T(2,128)S(1)} %get-tuple-element.127), channel_id=1, source_target_pairs={{0,16},{1,17},{2,18},{3,19},{4,20},{5,21},{6,22},{7,23},{8,24},{9,... | collective-permute-start | bytes 2312 | tf_op jit(solution)/shard_map/ppermute | solution.py:18
  6.2 24.6 %collective-permute-start.1 = (f32[3,1,2,32]{3,2,1,0:T(2,128)S(1)}, f32[3,1,2,32]{3,2,1,0:T(2,128)S(1)}, u32[]{:S(2)}, u32[]{:S(2)}) collective-permute-start(f32[3,1,2,32]{3,2,1,0:T(2,128)S(1)} %get-tuple-element.126), channel_id=1, source_target_pairs={{16,0},{17,1},{18,2},{19,3},{20,4},{21,5},{22,6},{23,7},{24,8},{25... | collective-permute-start | bytes 2312 | tf_op jit(solution)/shard_map/ppermute | solution.py:20
  8.8 44.9 %collective-permute-start.6 = (f32[2,8,128]{2,1,0:T(8,128)}, f32[2,8,128]{2,1,0:T(8,128)}, u32[]{:S(2)}, u32[]{:S(2)}) collective-permute-start(f32[2,8,128]{2,1,0:T(8,128)} %get-tuple-element.78), channel_id=1, source_target_pairs={{0,16},{1,17},{2,18},{3,19},{4,20},{5,21},{6,22},{7,23},{8,24},{9,... | collective-permute-start | bytes 24584 | tf_op jit(solution)/shard_map/ppermute | solution.py:18
  13.9 41.3 %collective-permute-start.7 = (f32[2,8,128]{2,1,0:T(8,128)}, f32[2,8,128]{2,1,0:T(8,128)}, u32[]{:S(2)}, u32[]{:S(2)}) collective-permute-start(f32[2,8,128]{2,1,0:T(8,128)} %get-tuple-element.77), channel_id=1, source_target_pairs={{16,0},{17,1},{18,2},{19,3},{20,4},{21,5},{22,6},{23,7},{24,8},{25... | collective-permute-start | bytes 24584 | tf_op jit(solution)/shard_map/ppermute | solution.py:20
  30.8 12.4 %collective-permute-start.2 = (f32[3,4,1,32]{3,2,1,0:T(1,128)S(1)}, f32[3,4,1,32]{3,2,1,0:T(1,128)S(1)}, u32[]{:S(2)}, u32[]{:S(2)}) collective-permute-start(f32[3,4,1,32]{3,2,1,0:T(1,128)S(1)} %get-tuple-element.85), channel_id=1, source_target_pairs={{0,4},{4,8},{8,12},{1,5},{5,9},{9,13},{2,6},{6,10},{10,14},{3,7},{... | collective-permute-start | bytes 4616 | tf_op jit(solution)/shard_map/ppermute | solution.py:18
  34.3 8.9 %collective-permute-start.3 = (f32[3,4,1,32]{3,2,1,0:T(1,128)S(1)}, f32[3,4,1,32]{3,2,1,0:T(1,128)S(1)}, u32[]{:S(2)}, u32[]{:S(2)}) collective-permute-start(f32[3,4,1,32]{3,2,1,0:T(1,128)S(1)} %get-tuple-element.86), channel_id=1, source_target_pairs={{4,0},{8,4},{12,8},{5,1},{9,5},{13,9},{6,2},{10,6},{14,10},{7,3},{... | collective-permute-start | bytes 4616 | tf_op jit(solution)/shard_map/ppermute | solution.py:20
  56.5 14.6 %collective-permute-start.8 = (f32[12,2,128]{2,1,0:T(2,128)}, f32[12,2,128]{2,1,0:T(2,128)}, u32[]{:S(2)}, u32[]{:S(2)}) collective-permute-start(f32[12,2,128]{2,1,0:T(2,128)} %get-tuple-element.72), channel_id=1, source_target_pairs={{0,4},{4,8},{8,12},{1,5},{5,9},{9,13},{2,6},{6,10},{10,14},{3,7},{... | collective-permute-start | bytes 36872 | tf_op jit(solution)/shard_map/ppermute | solution.py:18
  61.6 9.4 %collective-permute-start.9 = (f32[12,2,128]{2,1,0:T(2,128)}, f32[12,2,128]{2,1,0:T(2,128)}, u32[]{:S(2)}, u32[]{:S(2)}) collective-permute-start(f32[12,2,128]{2,1,0:T(2,128)} %get-tuple-element.73), channel_id=1, source_target_pairs={{4,0},{8,4},{12,8},{5,1},{9,5},{13,9},{6,2},{10,6},{14,10},{7,3},{... | collective-permute-start | bytes 36872 | tf_op jit(solution)/shard_map/ppermute | solution.py:20
  72.6 9.7 %collective-permute-start.10 = (f32[12,12,2]{2,1,0:T(8,128)}, f32[12,12,2]{2,1,0:T(8,128)}, u32[]{:S(2)}, u32[]{:S(2)}) collective-permute-start(f32[12,12,2]{2,1,0:T(8,128)} %get-tuple-element.66), channel_id=1, source_target_pairs={{0,1},{1,2},{2,3},{4,5},{5,6},{6,7},{8,9},{9,10},{10,11},{12,13},{... | collective-permute-start | bytes 3464 | tf_op jit(solution)/shard_map/ppermute | solution.py:18
  86.5 6.7 %collective-permute-start.12 = (f32[2,4,8,128]{3,2,1,0:T(8,128)S(1)}, f32[2,4,8,128]{3,2,1,0:T(8,128)S(1)}, u32[]{:S(2)}, u32[]{:S(2)}) collective-permute-start(f32[2,4,8,128]{3,2,1,0:T(8,128)S(1)} %get-tuple-element.70), channel_id=1, source_target_pairs={{0,16},{1,17},{2,18},{3,19},{4,20},{5,21},{6,22},{7,23},{8,24},{9,... | collective-permute-start | bytes 98312 | tf_op jit(solution)/shard_map/ppermute | solution.py:18
  91.7 6.0 %collective-permute-start.13 = (f32[2,4,8,128]{3,2,1,0:T(8,128)S(1)}, f32[2,4,8,128]{3,2,1,0:T(8,128)S(1)}, u32[]{:S(2)}, u32[]{:S(2)}) collective-permute-start(f32[2,4,8,128]{3,2,1,0:T(8,128)S(1)} %get-tuple-element.71), channel_id=1, source_target_pairs={{16,0},{17,1},{18,2},{19,3},{20,4},{21,5},{22,6},{23,7},{24,8},{25... | collective-permute-start | bytes 98312 | tf_op jit(solution)/shard_map/ppermute | solution.py:20
  97.8 6.2 %collective-permute-start.14 = (f32[2,16,4,128]{3,1,2,0:T(8,128)S(1)}, f32[2,16,4,128]{3,1,2,0:T(8,128)S(1)}, u32[]{:S(2)}, u32[]{:S(2)}) collective-permute-start(f32[2,16,4,128]{3,1,2,0:T(8,128)S(1)} %copy.1052), channel_id=1, source_target_pairs={{0,4},{4,8},{8,12},{1,5},{5,9},{9,13},{2,6},{6,10},{10,14},{3,7},{... | collective-permute-start | bytes 196616 | tf_op jit(solution)/shard_map/ppermute | solution.py:18
  102.1 6.2 %collective-permute-start.15 = (f32[2,16,4,128]{3,1,2,0:T(8,128)S(1)}, f32[2,16,4,128]{3,1,2,0:T(8,128)S(1)}, u32[]{:S(2)}, u32[]{:S(2)}) collective-permute-start(f32[2,16,4,128]{3,1,2,0:T(8,128)S(1)} %copy.1053), channel_id=1, source_target_pairs={{4,0},{8,4},{12,8},{5,1},{9,5},{13,9},{6,2},{10,6},{14,10},{7,3},{... | collective-permute-start | bytes 196616 | tf_op jit(solution)/shard_map/ppermute | solution.py:20
  109.8 5.6 %collective-permute-start.17 = (f32[2,16,16,4]{3,2,1,0:T(8,128)S(1)}, f32[2,16,16,4]{3,2,1,0:T(8,128)S(1)}, u32[]{:S(2)}, u32[]{:S(2)}) collective-permute-start(f32[2,16,16,4]{3,2,1,0:T(8,128)S(1)} %get-tuple-element.44), channel_id=1, source_target_pairs={{1,0},{2,1},{3,2},{5,4},{6,5},{7,6},{9,8},{10,9},{11,10},{13,12},{... | collective-permute-start | bytes 24584 | tf_op jit(solution)/shard_map/ppermute | solution.py:20
  118.0 10.0 %collective-permute-start.18 = (f32[3,4,8,128]{3,2,1,0:T(8,128)S(1)}, f32[3,4,8,128]{3,2,1,0:T(8,128)S(1)}, u32[]{:S(2)}, u32[]{:S(2)}) collective-permute-start(f32[3,4,8,128]{3,2,1,0:T(8,128)S(1)} %get-tuple-element.64), channel_id=1, source_target_pairs={{0,16},{1,17},{2,18},{3,19},{4,20},{5,21},{6,22},{7,23},{8,24},{9,... | collective-permute-start | bytes 147464 | tf_op jit(solution)/shard_map/ppermute | solution.py:18
  119.7 8.4 %collective-permute-start.19 = (f32[3,4,8,128]{3,2,1,0:T(8,128)S(1)}, f32[3,4,8,128]{3,2,1,0:T(8,128)S(1)}, u32[]{:S(2)}, u32[]{:S(2)}) collective-permute-start(f32[3,4,8,128]{3,2,1,0:T(8,128)S(1)} %get-tuple-element.65), channel_id=1, source_target_pairs={{16,0},{17,1},{18,2},{19,3},{20,4},{21,5},{22,6},{23,7},{24,8},{25... | collective-permute-start | bytes 147464 | tf_op jit(solution)/shard_map/ppermute | solution.py:20
  128.1 7.0 %collective-permute-start.20 = (f32[3,16,4,128]{3,1,2,0:T(8,128)S(1)}, f32[3,16,4,128]{3,1,2,0:T(8,128)S(1)}, u32[]{:S(2)}, u32[]{:S(2)}) collective-permute-start(f32[3,16,4,128]{3,1,2,0:T(8,128)S(1)} %copy.1054), channel_id=1, source_target_pairs={{0,4},{4,8},{8,12},{1,5},{5,9},{9,13},{2,6},{6,10},{10,14},{3,7},{... | collective-permute-start | bytes 294920 | tf_op jit(solution)/shard_map/ppermute | solution.py:18
  131.2 6.5 %collective-permute-start.21 = (f32[3,16,4,128]{3,1,2,0:T(8,128)S(1)}, f32[3,16,4,128]{3,1,2,0:T(8,128)S(1)}, u32[]{:S(2)}, u32[]{:S(2)}) collective-permute-start(f32[3,16,4,128]{3,1,2,0:T(8,128)S(1)} %copy.1055), channel_id=1, source_target_pairs={{4,0},{8,4},{12,8},{5,1},{9,5},{13,9},{6,2},{10,6},{14,10},{7,3},{... | collective-permute-start | bytes 294920 | tf_op jit(solution)/shard_map/ppermute | solution.py:20
  138.0 11.5 %collective-permute-start.22 = (f32[3,16,16,4]{3,2,1,0:T(8,128)S(1)}, f32[3,16,16,4]{3,2,1,0:T(8,128)S(1)}, u32[]{:S(2)}, u32[]{:S(2)}) collective-permute-start(f32[3,16,16,4]{3,2,1,0:T(8,128)S(1)} %get-tuple-element.41), channel_id=1, source_target_pairs={{0,1},{1,2},{2,3},{4,5},{5,6},{6,7},{8,9},{9,10},{10,11},{12,13},{... | collective-permute-start | bytes 36872 | tf_op jit(solution)/shard_map/ppermute | solution.py:18
  143.3 6.2 %collective-permute-start.23 = (f32[3,16,16,4]{3,2,1,0:T(8,128)S(1)}, f32[3,16,16,4]{3,2,1,0:T(8,128)}, u32[]{:S(2)}, u32[]{:S(2)}) collective-permute-start(f32[3,16,16,4]{3,2,1,0:T(8,128)S(1)} %get-tuple-element.42), channel_id=1, source_target_pairs={{1,0},{2,1},{3,2},{5,4},{6,5},{7,6},{9,8},{10,9},{11,10},{13,12},{... | collective-permute-start | bytes 36872 | tf_op jit(solution)/shard_map/ppermute | solution.py:20
  153.5 5.6 %collective-permute-start.24 = (f32[3,1,2,32]{3,2,1,0:T(2,128)S(1)}, f32[3,1,2,32]{3,2,1,0:T(2,128)S(1)}, u32[]{:S(2)}, u32[]{:S(2)}) collective-permute-start(f32[3,1,2,32]{3,2,1,0:T(2,128)S(1)} %get-tuple-element.91), channel_id=1, source_target_pairs={{0,16},{1,17},{2,18},{3,19},{4,20},{5,21},{6,22},{7,23},{8,24},{9,... | collective-permute-start | bytes 2312 | tf_op jit(solution)/shard_map/ppermute | solution.py:18
  163.3 48.6 %collective-permute-start.26 = (f32[3,4,1,32]{3,2,1,0:T(1,128)S(1)}, f32[3,4,1,32]{3,2,1,0:T(1,128)S(1)}, u32[]{:S(2)}, u32[]{:S(2)}) collective-permute-start(f32[3,4,1,32]{3,2,1,0:T(1,128)S(1)} %get-tuple-element.83), channel_id=1, source_target_pairs={{0,4},{4,8},{8,12},{1,5},{5,9},{9,13},{2,6},{6,10},{10,14},{3,7},{... | collective-permute-start | bytes 4616 | tf_op jit(solution)/shard_map/ppermute | solution.py:18
  167.0 44.9 %collective-permute-start.27 = (f32[3,4,1,32]{3,2,1,0:T(1,128)S(1)}, f32[3,4,1,32]{3,2,1,0:T(1,128)S(1)}, u32[]{:S(2)}, u32[]{:S(2)}) collective-permute-start(f32[3,4,1,32]{3,2,1,0:T(1,128)S(1)} %get-tuple-element.84), channel_id=1, source_target_pairs={{4,0},{8,4},{12,8},{5,1},{9,5},{13,9},{6,2},{10,6},{14,10},{7,3},{... | collective-permute-start | bytes 4616 | tf_op jit(solution)/shard_map/ppermute | solution.py:20
  213.3 5.8 %collective-permute-start.29 = (f32[3,4,4,1]{3,2,1,0:T(4,128)S(1)}, f32[3,4,4,1]{3,2,1,0:T(4,128)S(1)}, u32[]{:S(2)}, u32[]{:S(2)}) collective-permute-start(f32[3,4,4,1]{3,2,1,0:T(4,128)S(1)} %get-tuple-element.80), channel_id=1, source_target_pairs={{1,0},{2,1},{3,2},{5,4},{6,5},{7,6},{9,8},{10,9},{11,10},{13,12},{... | collective-permute-start | bytes 584 | tf_op jit(solution)/shard_map/ppermute | solution.py:20
  (91 other events, 460.1 us)
where the time goes:
time: 225 us; the launch traced here: 221 us
  starting transfers between devices  74.1 us (33%)
  local copies, waits for them, and re-layouts  51.2 us (23%)
  blocking collectives  43 us (19%)
  waiting for transfers between devices  26.8 us (12%)
  other arithmetic  20.8 us (9%)
  between operations  5.16 us (2%)
    ppermute x15, starting transfers between devices, extended(): lax.ppermute(tail, axis, [(i, (i + 1) % count) for i in range(ends)])  54.5 us
    psum x1, blocking collectives, on_device(): total = lax.psum(jnp.sum(similar), ('gx', 'gy', 'ga'))  43 us
    ppermute x15, waiting for transfers between devices, extended(): lax.ppermute(head, axis, [((i + 1) % count, i) for i in range(ends)])  25.9 us
    ppermute x15, starting transfers between devices, extended(): lax.ppermute(head, axis, [((i + 1) % count, i) for i in range(ends)])  19.5 us
    sub x33, local copies, waits for them, and re-layouts, shift_weights(): weights.append((lower * (1.0 - frac_k) + upper * frac_k, upper - lower))  11.2 us
    add x15, local copies, waits for them, and re-layouts, shift_weights(): weights.append((lower * (1.0 - frac_k) + upper * frac_k, upper - lower))  9.09 us
    eq x30, local copies, waits for them, and re-layouts, shift_weights(): lower = (offset_k == shift).astype(frac_k.dtype)  8.15 us
    eq x30, local copies, waits for them, and re-layouts, shift_weights(): upper = (offset_k + 1 == shift).astype(frac_k.dtype)  8.15 us
  transfers between devices with their start and end apart: 30, of which 9 were waited for; matrix products, arithmetic and copies ran while one was open for 25% of the time, Pallas kernels for 0%

commit v1 on v0

v1 whole, which is shorter than its diff:
```python
import functools
import jax
import jax.numpy as jnp
from jax import lax
from jax.experimental import pallas as pl
from jax.experimental.pallas import tpu as pltpu
from jax.sharding import PartitionSpec as P

window_count = 729.0
epsilon = 1e-05
MESH = pl.DeviceIdType.MESH
HIGHEST = lax.Precision.HIGHEST
PLANE = [(dx, dy) for dx in (-1, 0, 1) for dy in (-1, 0, 1) if (dx, dy) != (0, 0)]


def iota(shape, dim):
    return lax.broadcasted_iota(jnp.int32, shape, dim)


def dot(a, b):
    return jnp.dot(a, b, precision=HIGHEST, preferred_element_type=jnp.float32)


def as_float(mask):
    return jnp.where(mask, 1.0, 0.0).astype(jnp.float32)


def shifted(v, halo, s, lane):
    n = v.shape[-1]
    if s == 0:
        return v
    if s > 0:
        return pltpu.roll(jnp.where(lane < s, halo, v), n - s, v.ndim - 1)
    return pltpu.roll(jnp.where(lane >= n + s, halo, v), -s, v.ndim - 1)


def tent(diff):
    return jnp.where(diff == 0, 0.5, jnp.where(jnp.abs(diff) == 1, 0.25, 0.0))


def plane_filter():
    r = iota((16, 144), 0)
    c = iota((16, 144), 1)
    slot = c >> 4
    q = c & 15
    sx = jnp.where(slot >= 6, 2, jnp.where(slot >= 3, 1, 0))
    sy = slot - 3 * sx
    wx = tent(2 * sx + ((q >> 1) & 1) - 2 - ((r >> 1) & 1))
    wy = tent(2 * sy + (q & 1) - 2 - (r & 1))
    return jnp.where((r >> 2) == (q >> 2), wx * wy, 0.0).astype(jnp.float32)


def box_rows(v):
    s2 = v[:-1] + v[1:]
    s4 = s2[:-2] + s2[2:]
    s8 = s4[:-4] + s4[4:]
    return s8[:8] + v[8:16]


def kernel(sizes, count, fixed_ref, moving_ref, disp_ref, offs_ref, sim_ref, out_ref,
           cin, cup, cslot, gslot, gsrc, zc, zm, zf, zj, zk, zg, mext, fext, jext, cext, coef,
           shifts, slopes, smooth, offsets, tbox, tcoef, sims, send, recv):
    nx, ny, na = sizes
    me = {"gx": lax.axis_index("gx"), "gy": lax.axis_index("gy"), "ga": lax.axis_index("ga")}
    size = {"gx": nx, "gy": ny, "ga": na}
    pending = []
    counter = [0]

    def target(**moves):
        return {a: me[a] + moves.get(a, 0) for a in me}

    def exists(moves):
        conds = [((me[a] + d) >= 0) & ((me[a] + d) < size[a]) for a, d in moves.items() if d]
        return functools.reduce(jnp.logical_and, conds)

    def start(src, dst, moves):
        i = counter[0]
        counter[0] += 1
        c = pltpu.make_async_remote_copy(src, dst, send.at[i], recv.at[i],
                                         device_id=target(**moves), device_id_type=MESH)
        to = exists(moves)
        origin = exists({a: -d for a, d in moves.items()})
        pl.when(to)(c.start)
        pending.append((c, to))
        return c, origin

    def arrive(copies):
        for c, origin in copies:
            pl.when(origin)(c.wait_recv)

    def along(src, dst):
        return [start(src, dst.at[0], {"ga": 1}), start(src, dst.at[1], {"ga": -1})]

    def halo(z, lane):
        return jnp.where(lane < 64, z[1], z[0])

    def across(ext, lead, h):
        copies = []
        for dx, dy in PLANE:
            n = 8 if dx == 0 else h
            src0 = h + (8 - h if dx == 1 else 0)
            dst0 = {1: 0, 0: h, -1: h + 8}[dx]
            dsty = {1: 0, 0: 8, -1: 16}[dy]
            src = ext.at[lead, pl.ds(src0, n), pl.ds(8, 8), :]
            dst = ext.at[lead, pl.ds(dst0, n), pl.ds(dsty, 8), :]
            copies.append(start(src, dst, {"gx": dx, "gy": dy}))
        return copies

    def slots(ref):
        return [start(ref.at[4], ref.at[(1 - dx) * 3 + 1 - dy], {"gx": dx, "gy": dy}) for dx, dy in PLANE]

    def line(axis, base, tile):
        sims[base] = tile
        copies = []
        n = size[axis]
        for d in range(1, n):
            i = counter[0]
            counter[0] += 1
            dev = dict(me)
            dev[axis] = lax.rem(me[axis] + d, n)
            c = pltpu.make_async_remote_copy(sims.at[base], sims.at[base + d], send.at[i], recv.at[i],
                                             device_id=dev, device_id_type=MESH)
            c.start()
            pending.append((c, None))
            copies.append(c)
        return copies

    def line_sum(axis, base, copies):
        total = sims[base]
        for d, c in enumerate(copies):
            c.wait_recv()
            total = total + sims[base + 1 + d]
        return total

    for ref in (zc, zm, zf, zj, zk, zg, mext, fext, jext, cext, cslot, gslot, gsrc, cin):
        ref[...] = jnp.zeros(ref.shape, ref.dtype)

    barrier = pltpu.get_barrier_semaphore()
    expected = nx - 1 + ny - 1 + na - 1
    for axis in ("gx", "gy", "ga"):
        for d in range(1, size[axis]):
            dev = dict(me)
            dev[axis] = lax.rem(me[axis] + d, size[axis])
            pl.semaphore_signal(barrier, inc=1, device_id=dev, device_id_type=MESH)
    for dx, dy in PLANE:
        if dx and dy:
            moves = {"gx": dx, "gy": dy}
            cond = exists(moves)
            expected = expected + jnp.where(cond, 1, 0)

            def greet(moves=moves):
                pl.semaphore_signal(barrier, inc=1, device_id=target(**moves), device_id_type=MESH)

            pl.when(cond)(greet)

    for k in range(3):
        for cx in range(2):
            cin[0, pl.ds(4 * k + 2 * cx, 2), :] = disp_ref[k, cx]
            cin[1, pl.ds(4 * k + 2 * cx, 2), :] = offs_ref[k, cx].astype(jnp.float32)
    spread = as_float(iota((32, 128), 0) == (iota((32, 128), 1) >> 2))
    cup[0] = dot(cin[0], spread)
    offsets[...] = dot(cin[1], spread)
    mext[0, pl.ds(2, 8), pl.ds(8, 8), :] = moving_ref[...]
    fext[0, pl.ds(4, 8), pl.ds(8, 8), :] = fixed_ref[...]
    pl.semaphore_wait(barrier, expected)

    z_c = along(cup.at[0], zc)
    z_m = along(moving_ref, zm)
    m_center = across(mext, 0, 2)
    z_f = along(fixed_ref, zf)

    lane2 = iota((16, 128), 1)
    lane3 = iota((8, 8, 128), 2)
    arrive(z_c)
    u = cup[0]
    uh = halo(zc, lane2)
    cslot[4] = 0.25 * (shifted(u, uh, -4, lane2) + 2.0 * u + shifted(u, uh, 4, lane2))
    c_slots = slots(cslot)
    arrive(z_m)
    mext[1, pl.ds(2, 8), pl.ds(8, 8), :] = halo(zm, lane3)
    m_halo = across(mext, 1, 2)
    f_center = across(fext, 0, 4)
    arrive(z_f)
    fext[1, pl.ds(4, 8), pl.ds(8, 8), :] = halo(zf, lane3)
    f_halo = across(fext, 1, 4)

    filt = plane_filter()
    arrive(c_slots)
    smooth[...] = jax.nn.sigmoid(dot(filt, cslot[...].reshape(144, 128)))
    arrive(m_center)
    arrive(m_halo)
    lane_m = iota((12, 24, 128), 2)
    mv = mext[0]
    mh = mext[1]
    for iz in range(5):
        shifts[iz] = shifted(mv, mh, iz - 2, lane_m)

    low = iota((8, 128), 0) < 4

    def warp_row(r, carry):
        cx = r // 4
        weights = []
        for k in range(3):
            row = 4 * k + 2 * cx
            frac = jnp.where(low, smooth[pl.ds(row, 1), :], smooth[pl.ds(row + 1, 1), :])
            off = jnp.where(low, offsets[pl.ds(row, 1), :], offsets[pl.ds(row + 1, 1), :])
            pairs = []
            for shift in range(-2, 3):
                lower = off == float(shift)
                upper = off == float(shift - 1)
                w = jnp.where(lower, 1.0 - frac, jnp.where(upper, frac, 0.0))
                d = jnp.where(lower, -1.0, jnp.where(upper, 1.0, 0.0))
                pairs.append((w, d))
            weights.append(pairs)
        acc = None
        for ix in range(5):
            mid = None
            for iy in range(5):
                inner = None
                for iz in range(5):
                    v = shifts[iz, r + ix, pl.ds(6 + iy, 8), :]
                    wz, dz = weights[2][iz]
                    t = (wz * v, dz * v)
                    inner = t if inner is None else (inner[0] + t[0], inner[1] + t[1])
                wy, dy = weights[1][iy]
                t = (wy * inner[0], dy * inner[0], wy * inner[1])
                mid = t if mid is None else tuple(a + b for a, b in zip(mid, t))
            wx, dx = weights[0][ix]
            t = (wx * mid[0], dx * mid[0], wx * mid[1], wx * mid[2])
            acc = t if acc is None else tuple(a + b for a, b in zip(acc, t))
        jext[0, r + 4, pl.ds(8, 8), :] = acc[0]
        slopes[0, r] = acc[1]
        slopes[1, r] = acc[2]
        slopes[2, r] = acc[3]
        return carry

    lax.fori_loop(0, 8, warp_row, 0)

    z_j = along(jext.at[0, pl.ds(4, 8), pl.ds(8, 8), :], zj)
    j_center = across(jext, 0, 4)
    arrive(f_center)
    arrive(f_halo)
    for half in range(2):
        f = fext[half]
        tbox[0, half] = box_rows(f)
        tbox[2, half] = box_rows(f * f)
    arrive(z_j)
    jext[1, pl.ds(4, 8), pl.ds(8, 8), :] = halo(zj, lane3)
    j_halo = across(jext, 1, 4)
    zi = iota((256, 128), 0)
    zo = iota((256, 128), 1)
    band = as_float(((zi < 128) & (jnp.abs(zi - zo) <= 4))
                    | ((zi >= 128) & ((jnp.abs(zi - zo) <= 4) | (jnp.abs(zi - 256 - zo) <= 4))))

    def box_y(ref):
        total = ref[:, pl.ds(4, 8), :]
        for s in range(5, 13):
            total = total + ref[:, pl.ds(s, 8), :]
        return total

    arrive(j_center)
    arrive(j_halo)
    for half in range(2):
        f = fext[half]
        j = jext[half]
        tbox[1, half] = box_rows(j)
        tbox[3, half] = box_rows(j * j)
        tbox[4, half] = box_rows(f * j)
    sums = []
    for q in range(5):
        both = [box_y(tbox.at[q, half]).reshape(64, 128) for half in range(2)]
        sums.append(dot(jnp.concatenate(both, axis=1), band).reshape(8, 8, 128))
    fs, js = sums[0], sums[1]
    cross = sums[4] - fs * js / window_count
    fvar = sums[2] - fs * fs / window_count
    wvar = sums[3] - js * js / window_count
    den = fvar * wvar + epsilon
    inv = 1.0 / den
    ratio = cross * inv
    similar = cross * ratio
    ca = 2.0 * ratio
    cb = -(ratio * ratio) * fvar
    cc = -(ca * fs + 2.0 * cb * js) / window_count
    coef[0] = ca
    coef[1] = cb
    coef[2] = cc
    z_k = along(coef, zk)
    s_a = line("ga", 0, jnp.sum(similar, axis=0))
    arrive(z_k)
    for q in range(3):
        own = coef[q].reshape(64, 128)
        h = jnp.where(lane3 < 64, zk[1, q], zk[0, q]).reshape(64, 128)
        cext[q, pl.ds(4, 8), pl.ds(8, 8), :] = dot(jnp.concatenate([own, h], axis=1), band).reshape(8, 8, 128)
    c_copies = []
    for q in range(3):
        c_copies += across(cext, q, 4)
    s_x = line("gx", na, line_sum("ga", 0, s_a))
    arrive(c_copies)
    boxed = []
    for q in range(3):
        tcoef[q] = box_rows(cext[q])
    for q in range(3):
        boxed.append(box_y(tcoef.at[q]))
    grad = -(fixed_ref[...] * boxed[0] + 2.0 * jext[0, pl.ds(4, 8), pl.ds(8, 8), :] * boxed[1] + boxed[2])
    for k in range(3):
        t = grad * slopes[k]
        for cx in range(2):
            part = jnp.sum(t[4 * cx:4 * cx + 4], axis=0)
            for cy in range(2):
                row = jnp.sum(jnp.where(low == (cy == 0), part, 0.0), axis=0, keepdims=True)
                gsrc[pl.ds(4 * k + 2 * cx + cy, 1), :] = row
    group = as_float((iota((128, 128), 0) >> 2) == (iota((128, 128), 1) >> 2))
    s = smooth[...]
    u = dot(gsrc[...], group) * s * (1.0 - s)
    cup[1] = u
    z_g = along(cup.at[1], zg)
    s_y = line("gy", na + nx, line_sum("gx", na, s_x))
    arrive(z_g)
    uh = halo(zg, lane2)
    gslot[4] = 0.25 * (shifted(u, uh, -4, lane2) + 2.0 * u + shifted(u, uh, 4, lane2))
    g_slots = slots(gslot)
    total = line_sum("gy", na + nx, s_y)
    sim_ref[...] = (jnp.sum(total) / count).reshape(1, 1)
    arrive(g_slots)
    pick = as_float(iota((128, 32), 0) == (iota((128, 32), 1) << 2))
    final = dot(dot(filt, gslot[...].reshape(144, 128)), pick)
    for k in range(3):
        for cx in range(2):
            out_ref[k, cx] = final[4 * k + 2 * cx:4 * k + 2 * cx + 2]
    for c, to in pending:
        if to is None:
            c.wait_send()
        else:
            pl.when(to)(c.wait_send)


def solution(mesh):
    nx, ny, na = mesh.shape["gx"], mesh.shape["gy"], mesh.shape["ga"]

    def on_device(fixed, moving, disp, offs):
        count = float(fixed.size * nx * ny * na)
        f32 = jnp.float32
        vm = pltpu.VMEM
        copies = 160 + nx + ny + na
        sim, out = pl.pallas_call(
            functools.partial(kernel, (nx, ny, na), count),
            out_shape=(jax.ShapeDtypeStruct((1, 1), f32), jax.ShapeDtypeStruct(disp.shape, f32)),
            in_specs=[pl.BlockSpec(memory_space=pltpu.VMEM)] * 4,
            out_specs=(pl.BlockSpec(memory_space=pltpu.VMEM),) * 2,
            scratch_shapes=[
                vm((2, 16, 32), f32), vm((2, 16, 128), f32), vm((9, 16, 128), f32), vm((9, 16, 128), f32),
                vm((16, 128), f32), vm((2, 16, 128), f32), vm((2, 8, 8, 128), f32), vm((2, 8, 8, 128), f32),
                vm((2, 8, 8, 128), f32), vm((2, 3, 8, 8, 128), f32), vm((2, 16, 128), f32),
                vm((2, 12, 24, 128), f32), vm((2, 16, 24, 128), f32), vm((2, 16, 24, 128), f32),
                vm((3, 16, 24, 128), f32), vm((3, 8, 8, 128), f32), vm((5, 12, 24, 128), f32),
                vm((3, 8, 8, 128), f32), vm((16, 128), f32), vm((16, 128), f32),
                vm((5, 2, 8, 24, 128), f32), vm((3, 8, 24, 128), f32), vm((nx + ny + na, 8, 128), f32),
                pltpu.SemaphoreType.DMA((copies,)), pltpu.SemaphoreType.DMA((copies,)),
            ],
            compiler_params=pltpu.CompilerParams(
                collective_id=0, has_side_effects=True, vmem_limit_bytes=48 * 1024 * 1024),
        )(fixed, moving, disp, offs)
        return sim.reshape(()), out

    in_specs = (P("gx", "gy", "ga"), P("gx", "gy", "ga"), P(None, "gx", "gy", "ga"), P(None, "gx", "gy", "ga"))
    return jax.shard_map(on_device, mesh=mesh, in_specs=in_specs,
                         out_specs=(P(), P(None, "gx", "gy", "ga")), check_vma=False)
```

time: 225 us -> 41.2 us (0.18); the launches traced: 221 us -> 40.8 us
  starting transfers between devices: 74.1 us -> 0 us
  local copies, waits for them, and re-layouts: 51.2 us -> 3.49 us
  blocking collectives: 43 us -> 0 us
  Pallas kernels: 0 us -> 35 us
  waiting for transfers between devices: 26.8 us -> 0 us
  other arithmetic: 20.8 us -> 0 us
  between operations: 5.16 us -> 2.4 us
    ppermute x30 -> x0, starting transfers between devices: 74.1 us -> none  [the longest x15 54.5 us: extended(): lax.ppermute(tail, axis, [(i, (i + 1) % count) for i in range(ends)])]
    psum x1 -> x0, blocking collectives: 43 us -> none  [on_device(): total = lax.psum(jnp.sum(similar), ('gx', 'gy', 'ga'))]
    pallas_call x0 -> x1, Pallas kernels: none -> 35 us  [on_device(): pl.pallas_call(functools.partial(kernel, (nx, ny, na), count), out_shape=...]
    ppermute x30 -> x0, waiting for transfers between devices: 26.8 us -> none  [the longest x15 25.9 us: extended(): lax.ppermute(head, axis, [((i + 1) % count, i) for i in range(ends)])]
    eq x60 -> x0, local copies, waits for them, and re-layouts: 16.3 us -> none  [the longest x30 8.15 us: shift_weights(): lower = (offset_k == shift).astype(frac_k.dtype)]
    add x13 -> x0, other arithmetic: 11.8 us -> none  [the longest x3 4.81 us: shift_weights(): weights.append((lower * (1.0 - frac_k) + upper * frac_k, upper - lower))]
    sub x33 -> x0, local copies, waits for them, and re-layouts: 11.2 us -> none  [shift_weights(): weights.append((lower * (1.0 - frac_k) + upper * frac_k, upper - lower))]
    add x15 -> x0, local copies, waits for them, and re-layouts: 9.09 us -> none  [shift_weights(): weights.append((lower * (1.0 - frac_k) + upper * frac_k, upper - lower))]
  transfers between devices with their start and end apart: 30 -> 0, of which waited for: 9 -> 0; matrix products, arithmetic and copies ran while one was open for 25% -> 0% of each run, Pallas kernels for 0% -> 0%
where the time goes in v1:
time: 41.2 us; the launch traced here: 40.8 us
  Pallas kernels  35 us (85%)
  local copies, waits for them, and re-layouts  3.49 us (8%)
  between operations  2.4 us (6%)
    pallas_call x1, Pallas kernels, on_device(): pl.pallas_call(functools.partial(kernel, (nx, ny, na), count), out_shape=...  35 us
    unnamed x9, local copies, waits for them, and re-layouts  3.49 us

profile of v1, /device:TPU:0, one launch (start us, length us, event | category | flops | bytes accessed | tf_op | source)
XLA Modules:
  0.0 40.8 jit_solution(13426409838046888561)
XLA Ops:
  0.6 0.0 copy-start
  0.6 0.7 %copy-done = f32[8,8,128]{2,1,0:T(8,128)S(1)} copy-done((f32[8,8,128]{2,1,0:T(8,128)S(1)}, f32[8,8,128]{2,1,0:T(8,128)}, u32[]{:S(2)}) %copy-start) | copy-done | bytes 32792
  1.4 0.0 copy-start.1
  1.4 0.8 %copy-done.1 = f32[8,8,128]{2,1,0:T(8,128)S(1)} copy-done((f32[8,8,128]{2,1,0:T(8,128)S(1)}, f32[8,8,128]{2,1,0:T(8,128)}, u32[]{:S(2)}) %copy-start.1) | copy-done | bytes 32792
  2.1 0.0 copy-start.2
  2.1 0.7 %copy-done.2 = f32[3,2,2,32]{3,2,1,0:T(2,128)S(1)} copy-done((f32[3,2,2,32]{3,2,1,0:T(2,128)S(1)}, f32[3,2,2,32]{3,2,1,0:T(2,128)}, u32[]{:S(2)}) %copy-start.2) | copy-done | bytes 1560
  2.8 0.0 copy-start.3
  2.8 0.7 %copy-done.3 = s32[3,2,2,32]{3,2,1,0:T(2,128)S(1)} copy-done((s32[3,2,2,32]{3,2,1,0:T(2,128)S(1)}, s32[3,2,2,32]{3,2,1,0:T(2,128)}, u32[]{:S(2)}) %copy-start.3) | copy-done | bytes 1560
  3.5 35.0 %shard_map.59 = (f32[1,1]{1,0:T(1,128)}, f32[3,2,2,32]{3,2,1,0:T(2,128)S(1)}) custom-call(f32[8,8,128]{2,1,0:T(8,128)S(1)} %copy-done, f32[8,8,128]{2,1,0:T(8,128)S(1)} %copy-done.1, f32[3,2,2,32]{3,2,1,0:T(2,128)S(1)} %copy-done.2, s32[3,2,2,32]{3,2,1,0:T(2,128)S(1)} %copy-done.3), custom_call_target="tpu_custom_call" | custom-call | tf_op jit(solution)/shard_map/pallas_call | solution.py:345
  39.1 0.6 %copy.9 = f32[3,2,2,32]{3,2,1,0:T(2,128)} copy(f32[3,2,2,32]{3,2,1,0:T(2,128)S(1)} %get-tuple-element.9) | data formatting | bytes 3072
Async XLA Ops:
  0.6 0.8 %copy-start = (f32[8,8,128]{2,1,0:T(8,128)S(1)}, f32[8,8,128]{2,1,0:T(8,128)}, u32[]{:S(2)}) copy-start(f32[8,8,128]{2,1,0:T(8,128)} %fixed_ref.1) | copy-start | bytes 98308
  1.4 0.8 %copy-start.1 = (f32[8,8,128]{2,1,0:T(8,128)S(1)}, f32[8,8,128]{2,1,0:T(8,128)}, u32[]{:S(2)}) copy-start(f32[8,8,128]{2,1,0:T(8,128)} %moving_ref.1) | copy-start | bytes 98308
  2.1 0.7 %copy-start.2 = (f32[3,2,2,32]{3,2,1,0:T(2,128)S(1)}, f32[3,2,2,32]{3,2,1,0:T(2,128)}, u32[]{:S(2)}) copy-start(f32[3,2,2,32]{3,2,1,0:T(2,128)} %disp_ref.1) | copy-start | bytes 4612
  2.8 0.7 %copy-start.3 = (s32[3,2,2,32]{3,2,1,0:T(2,128)S(1)}, s32[3,2,2,32]{3,2,1,0:T(2,128)}, u32[]{:S(2)}) copy-start(s32[3,2,2,32]{3,2,1,0:T(2,128)} %offs_ref.1) | copy-start | bytes 4612

commit v2 on v1

--- a/solution.py
+++ b/solution.py
@@ -58,7 +58,7 @@
 
 
 def kernel(sizes, count, fixed_ref, moving_ref, disp_ref, offs_ref, sim_ref, out_ref,
-           cin, cup, cslot, gslot, gsrc, zc, zm, zf, zj, zk, zg, mext, fext, jext, cext, coef,
+           cin, cup, cslot, gslot, gsrc, zc, zg, edge, zedge, qi, qj, hm, hf, hj, hk, mext, fext, jext, cext, coef,
            shifts, slopes, smooth, offsets, tbox, tcoef, sims, send, recv):
     nx, ny, na = sizes
     me = {"gx": lax.axis_index("gx"), "gy": lax.axis_index("gy"), "ga": lax.axis_index("ga")}
@@ -100,9 +100,11 @@
             n = 8 if dx == 0 else h
             src0 = h + (8 - h if dx == 1 else 0)
             dst0 = {1: 0, 0: h, -1: h + 8}[dx]
-            dsty = {1: 0, 0: 8, -1: 16}[dy]
-            src = ext.at[lead, pl.ds(src0, n), pl.ds(8, 8), :]
-            dst = ext.at[lead, pl.ds(dst0, n), pl.ds(dsty, 8), :]
+            wide = 8 if dy == 0 else 4
+            srcy = 12 if dy == 1 else 8
+            dsty = {1: 4, 0: 8, -1: 16}[dy]
+            src = ext.at[lead, pl.ds(src0, n), pl.ds(srcy, wide), :]
+            dst = ext.at[lead, pl.ds(dst0, n), pl.ds(dsty, wide), :]
             copies.append(start(src, dst, {"gx": dx, "gy": dy}))
         return copies
 
@@ -132,7 +134,28 @@
             total = total + sims[base + 1 + d]
         return total
 
-    for ref in (zc, zm, zf, zj, zk, zg, mext, fext, jext, cext, cslot, gslot, gsrc, cin):
+    lane1 = iota((8, 128), 1)
+
+    def pack(rows):
+        tile = jnp.zeros((8, 128), jnp.float32)
+        for i, v in enumerate(rows):
+            tile = jnp.where((lane1 >> 3) == i, pltpu.roll(v, (4 + 8 * i) % 128, 1), tile)
+        return tile
+
+    def merged(i):
+        return jnp.where((lane1 & 7) < 4, zedge[i, 0], zedge[i, 1])
+
+    def unpack(tile, i):
+        return pltpu.roll(tile, (124 - 8 * i) % 128, 1)
+
+    def halo_rows(ref, q, h, first):
+        for sy in range(3):
+            for sx, x0, n, d0 in ((0, 8 - h, h, 0), (1, 0, 8, h), (2, 0, h, h + 8)):
+                tile = q[3 * sx + sy]
+                for x in range(n):
+                    ref[d0 + x, pl.ds(8 * sy, 8), :] = unpack(tile, first + x0 + x)
+
+    for ref in (zc, zg, zedge, qi, qj, mext, fext, jext, cext, cslot, gslot, gsrc, cin):
         ref[...] = jnp.zeros(ref.shape, ref.dtype)
 
     barrier = pltpu.get_barrier_semaphore()
@@ -161,37 +184,34 @@
     cup[0] = dot(cin[0], spread)
     offsets[...] = dot(cin[1], spread)
     mext[0, pl.ds(2, 8), pl.ds(8, 8), :] = moving_ref[...]
+    edge[0] = pack([moving_ref[i] for i in range(8)] + [fixed_ref[i] for i in range(8)])
     fext[0, pl.ds(4, 8), pl.ds(8, 8), :] = fixed_ref[...]
     pl.semaphore_wait(barrier, expected)
 
     z_c = along(cup.at[0], zc)
-    z_m = along(moving_ref, zm)
+    z_i = along(edge.at[0], zedge.at[0])
     m_center = across(mext, 0, 2)
-    z_f = along(fixed_ref, zf)
+    f_center = across(fext, 0, 4)
 
     lane2 = iota((16, 128), 1)
-    lane3 = iota((8, 8, 128), 2)
     arrive(z_c)
     u = cup[0]
     uh = halo(zc, lane2)
     cslot[4] = 0.25 * (shifted(u, uh, -4, lane2) + 2.0 * u + shifted(u, uh, 4, lane2))
     c_slots = slots(cslot)
-    arrive(z_m)
-    mext[1, pl.ds(2, 8), pl.ds(8, 8), :] = halo(zm, lane3)
-    m_halo = across(mext, 1, 2)
-    f_center = across(fext, 0, 4)
-    arrive(z_f)
-    fext[1, pl.ds(4, 8), pl.ds(8, 8), :] = halo(zf, lane3)
-    f_halo = across(fext, 1, 4)
+    arrive(z_i)
+    qi[4] = merged(0)
+    i_slots = slots(qi)
 
     filt = plane_filter()
     arrive(c_slots)
     smooth[...] = jax.nn.sigmoid(dot(filt, cslot[...].reshape(144, 128)))
+    arrive(i_slots)
+    halo_rows(hm, qi, 2, 0)
     arrive(m_center)
-    arrive(m_halo)
     lane_m = iota((12, 24, 128), 2)
     mv = mext[0]
-    mh = mext[1]
+    mh = hm[...]
     for iz in range(5):
         shifts[iz] = shifted(mv, mh, iz - 2, lane_m)
 
@@ -236,17 +256,18 @@
 
     lax.fori_loop(0, 8, warp_row, 0)
 
-    z_j = along(jext.at[0, pl.ds(4, 8), pl.ds(8, 8), :], zj)
+    edge[1] = pack([jext[0, 4 + i, pl.ds(8, 8), :] for i in range(8)])
+    z_j = along(edge.at[1], zedge.at[1])
     j_center = across(jext, 0, 4)
+    arrive(z_j)
+    qj[4] = merged(1)
+    j_slots = slots(qj)
+    halo_rows(hf, qi, 4, 8)
     arrive(f_center)
-    arrive(f_halo)
     for half in range(2):
-        f = fext[half]
+        f = (fext[0], hf[...])[half]
         tbox[0, half] = box_rows(f)
         tbox[2, half] = box_rows(f * f)
-    arrive(z_j)
-    jext[1, pl.ds(4, 8), pl.ds(8, 8), :] = halo(zj, lane3)
-    j_halo = across(jext, 1, 4)
     zi = iota((256, 128), 0)
     zo = iota((256, 128), 1)
     band = as_float(((zi < 128) & (jnp.abs(zi - zo) <= 4))
@@ -258,11 +279,12 @@
             total = total + ref[:, pl.ds(s, 8), :]
         return total
 
+    arrive(j_slots)
+    halo_rows(hj, qj, 4, 0)
     arrive(j_center)
-    arrive(j_halo)
     for half in range(2):
-        f = fext[half]
-        j = jext[half]
+        f = (fext[0], hf[...])[half]
+        j = (jext[0], hj[...])[half]
         tbox[1, half] = box_rows(j)
         tbox[3, half] = box_rows(j * j)
         tbox[4, half] = box_rows(f * j)
@@ -284,12 +306,18 @@
     coef[0] = ca
     coef[1] = cb
     coef[2] = cc
-    z_k = along(coef, zk)
+    rows = [ca[i] for i in range(8)] + [cb[i] for i in range(8)]
+    edge[2] = pack(rows)
+    edge[3] = pack([cc[i] for i in range(8)])
+    z_k = along(edge.at[2], zedge.at[2]) + along(edge.at[3], zedge.at[3])
     s_a = line("ga", 0, jnp.sum(similar, axis=0))
     arrive(z_k)
     for q in range(3):
         own = coef[q].reshape(64, 128)
-        h = jnp.where(lane3 < 64, zk[1, q], zk[0, q]).reshape(64, 128)
+        tile = merged(2 + q // 2)
+        for x in range(8):
+            hk[x] = unpack(tile, 8 * (q % 2) + x)
+        h = hk[...].reshape(64, 128)
         cext[q, pl.ds(4, 8), pl.ds(8, 8), :] = dot(jnp.concatenate([own, h], axis=1), band).reshape(8, 8, 128)
     c_copies = []
     for q in range(3):
@@ -349,9 +377,10 @@
             out_specs=(pl.BlockSpec(memory_space=pltpu.VMEM),) * 2,
             scratch_shapes=[
                 vm((2, 16, 32), f32), vm((2, 16, 128), f32), vm((9, 16, 128), f32), vm((9, 16, 128), f32),
-                vm((16, 128), f32), vm((2, 16, 128), f32), vm((2, 8, 8, 128), f32), vm((2, 8, 8, 128), f32),
-                vm((2, 8, 8, 128), f32), vm((2, 3, 8, 8, 128), f32), vm((2, 16, 128), f32),
-                vm((2, 12, 24, 128), f32), vm((2, 16, 24, 128), f32), vm((2, 16, 24, 128), f32),
+                vm((16, 128), f32), vm((2, 16, 128), f32), vm((2, 16, 128), f32),
+                vm((4, 8, 128), f32), vm((4, 2, 8, 128), f32), vm((9, 8, 128), f32), vm((9, 8, 128), f32),
+                vm((12, 24, 128), f32), vm((16, 24, 128), f32), vm((16, 24, 128), f32), vm((8, 8, 128), f32),
+                vm((1, 12, 24, 128), f32), vm((1, 16, 24, 128), f32), vm((1, 16, 24, 128), f32),
                 vm((3, 16, 24, 128), f32), vm((3, 8, 8, 128), f32), vm((5, 12, 24, 128), f32),
                 vm((3, 8, 8, 128), f32), vm((16, 128), f32), vm((16, 128), f32),
                 vm((5, 2, 8, 24, 128), f32), vm((3, 8, 24, 128), f32), vm((nx + ny + na, 8, 128), f32),

time: 41.2 us -> 39 us (0.947)
  Pallas kernels: 35 us -> 32.8 us
    pallas_call x1, Pallas kernels: 35 us -> 32.8 us  [on_device(): pl.pallas_call(functools.partial(kernel, (nx, ny, na), count), out_shape=...]
where the time goes in v2:
time: 39 us; the launch traced here: 38.7 us
  Pallas kernels  32.8 us (84%)
  local copies, waits for them, and re-layouts  3.49 us (9%)
  between operations  2.4 us (6%)
    pallas_call x1, Pallas kernels, on_device(): pl.pallas_call(functools.partial(kernel, (nx, ny, na), count), out_shape=...  32.8 us
    unnamed x9, local copies, waits for them, and re-layouts  3.49 us

profile of v2, /device:TPU:0, one launch (start us, length us, event | category | flops | bytes accessed | tf_op | source)
XLA Modules:
  0.0 38.7 jit_solution(3475275937024396455)
XLA Ops:
  0.6 0.0 copy-start
  0.6 0.7 %copy-done = f32[8,8,128]{2,1,0:T(8,128)S(1)} copy-done((f32[8,8,128]{2,1,0:T(8,128)S(1)}, f32[8,8,128]{2,1,0:T(8,128)}, u32[]{:S(2)}) %copy-start) | copy-done | bytes 32792
  1.4 0.0 copy-start.1
  1.4 0.8 %copy-done.1 = f32[8,8,128]{2,1,0:T(8,128)S(1)} copy-done((f32[8,8,128]{2,1,0:T(8,128)S(1)}, f32[8,8,128]{2,1,0:T(8,128)}, u32[]{:S(2)}) %copy-start.1) | copy-done | bytes 32792
  2.1 0.0 copy-start.2
  2.1 0.7 %copy-done.2 = f32[3,2,2,32]{3,2,1,0:T(2,128)S(1)} copy-done((f32[3,2,2,32]{3,2,1,0:T(2,128)S(1)}, f32[3,2,2,32]{3,2,1,0:T(2,128)}, u32[]{:S(2)}) %copy-start.2) | copy-done | bytes 1560
  2.8 0.0 copy-start.3
  2.8 0.7 %copy-done.3 = s32[3,2,2,32]{3,2,1,0:T(2,128)S(1)} copy-done((s32[3,2,2,32]{3,2,1,0:T(2,128)S(1)}, s32[3,2,2,32]{3,2,1,0:T(2,128)}, u32[]{:S(2)}) %copy-start.3) | copy-done | bytes 1560
  3.5 32.8 %shard_map.59 = (f32[1,1]{1,0:T(1,128)}, f32[3,2,2,32]{3,2,1,0:T(2,128)S(1)}) custom-call(f32[8,8,128]{2,1,0:T(8,128)S(1)} %copy-done, f32[8,8,128]{2,1,0:T(8,128)S(1)} %copy-done.1, f32[3,2,2,32]{3,2,1,0:T(2,128)S(1)} %copy-done.2, s32[3,2,2,32]{3,2,1,0:T(2,128)S(1)} %copy-done.3), custom_call_target="tpu_custom_call" | custom-call | tf_op jit(solution)/shard_map/pallas_call | solution.py:373
  36.9 0.6 %copy.9 = f32[3,2,2,32]{3,2,1,0:T(2,128)} copy(f32[3,2,2,32]{3,2,1,0:T(2,128)S(1)} %get-tuple-element.9) | data formatting | bytes 3072
Async XLA Ops:
  0.6 0.8 %copy-start = (f32[8,8,128]{2,1,0:T(8,128)S(1)}, f32[8,8,128]{2,1,0:T(8,128)}, u32[]{:S(2)}) copy-start(f32[8,8,128]{2,1,0:T(8,128)} %fixed_ref.1) | copy-start | bytes 98308
  1.4 0.8 %copy-start.1 = (f32[8,8,128]{2,1,0:T(8,128)S(1)}, f32[8,8,128]{2,1,0:T(8,128)}, u32[]{:S(2)}) copy-start(f32[8,8,128]{2,1,0:T(8,128)} %moving_ref.1) | copy-start | bytes 98308
  2.1 0.7 %copy-start.2 = (f32[3,2,2,32]{3,2,1,0:T(2,128)S(1)}, f32[3,2,2,32]{3,2,1,0:T(2,128)}, u32[]{:S(2)}) copy-start(f32[3,2,2,32]{3,2,1,0:T(2,128)} %disp_ref.1) | copy-start | bytes 4612
  2.8 0.7 %copy-start.3 = (s32[3,2,2,32]{3,2,1,0:T(2,128)S(1)}, s32[3,2,2,32]{3,2,1,0:T(2,128)}, u32[]{:S(2)}) copy-start(s32[3,2,2,32]{3,2,1,0:T(2,128)} %offs_ref.1) | copy-start | bytes 4612

commit v3 on v2

--- a/solution.py
+++ b/solution.py
@@ -10,6 +10,7 @@
 epsilon = 1e-05
 MESH = pl.DeviceIdType.MESH
 HIGHEST = lax.Precision.HIGHEST
+NINE = [(dx, dy) for dx in (0, -1, 1) for dy in (0, -1, 1)]
 PLANE = [(dx, dy) for dx in (-1, 0, 1) for dy in (-1, 0, 1) if (dx, dy) != (0, 0)]
 
 
@@ -57,8 +58,9 @@
     return s8[:8] + v[8:16]
 
 
-def kernel(sizes, count, fixed_ref, moving_ref, disp_ref, offs_ref, sim_ref, out_ref,
-           cin, cup, cslot, gslot, gsrc, zc, zg, edge, zedge, qi, qj, hm, hf, hj, hk, mext, fext, jext, cext, coef,
+def kernel(sizes, count, fixed_any, moving_any, disp_any, offs_any, sim_ref, out_ref,
+           fixed_ref, moving_ref, disp_ref, offs_ref, local,
+           cin, cslot, gslot, gsrc, edge_i, edge_j, edge_k, edge_g, zi_, zj_, zk_, zg_, hm, hf, hj, hk, mext, fext, jext, cext,
            shifts, slopes, smooth, offsets, tbox, tcoef, sims, send, recv):
     nx, ny, na = sizes
     me = {"gx": lax.axis_index("gx"), "gy": lax.axis_index("gy"), "ga": lax.axis_index("ga")}
@@ -89,10 +91,8 @@
             pl.when(origin)(c.wait_recv)
 
     def along(src, dst):
-        return [start(src, dst.at[0], {"ga": 1}), start(src, dst.at[1], {"ga": -1})]
-
-    def halo(z, lane):
-        return jnp.where(lane < 64, z[1], z[0])
+        return [start(src, dst.at[i, (1 - dx) * 3 + 1 - dy], {"gx": dx, "gy": dy, "ga": dz})
+                for dx, dy in NINE for i, dz in ((0, 1), (1, -1))]
 
     def across(ext, lead, h):
         copies = []
@@ -143,7 +143,10 @@
         return tile
 
     def merged(i):
-        return jnp.where((lane1 & 7) < 4, zedge[i, 0], zedge[i, 1])
+        z, part = i
+        if part is None:
+            return lambda q: jnp.where((lane1 & 7) < 4, z[0, q], z[1, q])
+        return lambda q: jnp.where((lane1 & 7) < 4, z[0, q, part], z[1, q, part])
 
     def unpack(tile, i):
         return pltpu.roll(tile, (124 - 8 * i) % 128, 1)
@@ -151,11 +154,26 @@
     def halo_rows(ref, q, h, first):
         for sy in range(3):
             for sx, x0, n, d0 in ((0, 8 - h, h, 0), (1, 0, 8, h), (2, 0, h, h + 8)):
-                tile = q[3 * sx + sy]
+                tile = q(3 * sx + sy)
                 for x in range(n):
                     ref[d0 + x, pl.ds(8 * sy, 8), :] = unpack(tile, first + x0 + x)
 
-    for ref in (zc, zg, zedge, qi, qj, mext, fext, jext, cext, cslot, gslot, gsrc, cin):
+    def smooth_z(slots_ref, q):
+        rows = []
+        for slot in range(9):
+            tile = q(slot)
+            u = slots_ref[slot]
+            uh = jnp.concatenate([unpack(tile, 0), unpack(tile, 1)], axis=0)
+            rows.append(0.25 * (shifted(u, uh, -4, lane2) + 2.0 * u + shifted(u, uh, 4, lane2)))
+        return jnp.concatenate(rows, axis=0)
+
+    loads = [pltpu.make_async_copy(a, b, local.at[i]) for i, (a, b) in enumerate(
+        ((disp_any, disp_ref), (offs_any, offs_ref), (moving_any, moving_ref), (fixed_any, fixed_ref)))]
+    for c in loads:
+        c.start()
+    lane2 = iota((16, 128), 1)
+
+    for ref in (zi_, zj_, zk_, zg_, mext, fext, jext, cext, cslot, gslot, gsrc, cin):
         ref[...] = jnp.zeros(ref.shape, ref.dtype)
 
     barrier = pltpu.get_barrier_semaphore()
@@ -165,9 +183,11 @@
             dev = dict(me)
             dev[axis] = lax.rem(me[axis] + d, size[axis])
             pl.semaphore_signal(barrier, inc=1, device_id=dev, device_id_type=MESH)
-    for dx, dy in PLANE:
-        if dx and dy:
-            moves = {"gx": dx, "gy": dy}
+    for dx, dy in NINE:
+        for dz in (-1, 0, 1):
+            if (dx != 0) + (dy != 0) + (dz != 0) < 2:
+                continue
+            moves = {"gx": dx, "gy": dy, "ga": dz}
             cond = exists(moves)
             expected = expected + jnp.where(cond, 1, 0)
 
@@ -176,38 +196,30 @@
 
             pl.when(cond)(greet)
 
+    for c in loads:
+        c.wait()
     for k in range(3):
         for cx in range(2):
             cin[0, pl.ds(4 * k + 2 * cx, 2), :] = disp_ref[k, cx]
             cin[1, pl.ds(4 * k + 2 * cx, 2), :] = offs_ref[k, cx].astype(jnp.float32)
     spread = as_float(iota((32, 128), 0) == (iota((32, 128), 1) >> 2))
-    cup[0] = dot(cin[0], spread)
+    cslot[4] = dot(cin[0], spread)
     offsets[...] = dot(cin[1], spread)
     mext[0, pl.ds(2, 8), pl.ds(8, 8), :] = moving_ref[...]
-    edge[0] = pack([moving_ref[i] for i in range(8)] + [fixed_ref[i] for i in range(8)])
+    edge_i[1] = pack([cslot[4, 0:8], cslot[4, 8:16]])
+    edge_i[0] = pack([moving_ref[i] for i in range(8)] + [fixed_ref[i] for i in range(8)])
     fext[0, pl.ds(4, 8), pl.ds(8, 8), :] = fixed_ref[...]
     pl.semaphore_wait(barrier, expected)
 
-    z_c = along(cup.at[0], zc)
-    z_i = along(edge.at[0], zedge.at[0])
+    z_i = along(edge_i, zi_)
+    c_slots = slots(cslot)
     m_center = across(mext, 0, 2)
     f_center = across(fext, 0, 4)
-
-    lane2 = iota((16, 128), 1)
-    arrive(z_c)
-    u = cup[0]
-    uh = halo(zc, lane2)
-    cslot[4] = 0.25 * (shifted(u, uh, -4, lane2) + 2.0 * u + shifted(u, uh, 4, lane2))
-    c_slots = slots(cslot)
-    arrive(z_i)
-    qi[4] = merged(0)
-    i_slots = slots(qi)
-
     filt = plane_filter()
     arrive(c_slots)
-    smooth[...] = jax.nn.sigmoid(dot(filt, cslot[...].reshape(144, 128)))
-    arrive(i_slots)
-    halo_rows(hm, qi, 2, 0)
+    arrive(z_i)
+    smooth[...] = jax.nn.sigmoid(dot(filt, smooth_z(cslot, merged((zi_, 1)))))
+    halo_rows(hm, merged((zi_, 0)), 2, 0)
     arrive(m_center)
     lane_m = iota((12, 24, 128), 2)
     mv = mext[0]
@@ -256,13 +268,10 @@
 
     lax.fori_loop(0, 8, warp_row, 0)
 
-    edge[1] = pack([jext[0, 4 + i, pl.ds(8, 8), :] for i in range(8)])
-    z_j = along(edge.at[1], zedge.at[1])
+    edge_j[...] = pack([jext[0, 4 + i, pl.ds(8, 8), :] for i in range(8)])
+    z_j = along(edge_j, zj_)
     j_center = across(jext, 0, 4)
-    arrive(z_j)
-    qj[4] = merged(1)
-    j_slots = slots(qj)
-    halo_rows(hf, qi, 4, 8)
+    halo_rows(hf, merged((zi_, 0)), 4, 8)
     arrive(f_center)
     for half in range(2):
         f = (fext[0], hf[...])[half]
@@ -279,8 +288,8 @@
             total = total + ref[:, pl.ds(s, 8), :]
         return total
 
-    arrive(j_slots)
-    halo_rows(hj, qj, 4, 0)
+    arrive(z_j)
+    halo_rows(hj, merged((zj_, None)), 4, 0)
     arrive(j_center)
     for half in range(2):
         f = (fext[0], hf[...])[half]
@@ -303,32 +312,27 @@
     ca = 2.0 * ratio
     cb = -(ratio * ratio) * fvar
     cc = -(ca * fs + 2.0 * cb * js) / window_count
-    coef[0] = ca
-    coef[1] = cb
-    coef[2] = cc
     rows = [ca[i] for i in range(8)] + [cb[i] for i in range(8)]
-    edge[2] = pack(rows)
-    edge[3] = pack([cc[i] for i in range(8)])
-    z_k = along(edge.at[2], zedge.at[2]) + along(edge.at[3], zedge.at[3])
+    edge_k[0] = pack(rows)
+    edge_k[1] = pack([cc[i] for i in range(8)])
+    z_k = along(edge_k, zk_)
+    c_copies = []
+    for q, v in enumerate((ca, cb, cc)):
+        cext[q, pl.ds(4, 8), pl.ds(8, 8), :] = v
+        c_copies += across(cext, q, 4)
     s_a = line("ga", 0, jnp.sum(similar, axis=0))
+    s_x = line("gx", na, line_sum("ga", 0, s_a))
     arrive(z_k)
     for q in range(3):
-        own = coef[q].reshape(64, 128)
-        tile = merged(2 + q // 2)
-        for x in range(8):
-            hk[x] = unpack(tile, 8 * (q % 2) + x)
-        h = hk[...].reshape(64, 128)
-        cext[q, pl.ds(4, 8), pl.ds(8, 8), :] = dot(jnp.concatenate([own, h], axis=1), band).reshape(8, 8, 128)
-    c_copies = []
-    for q in range(3):
-        c_copies += across(cext, q, 4)
-    s_x = line("gx", na, line_sum("ga", 0, s_a))
+        halo_rows(hk.at[q], merged((zk_, q // 2)), 4, 8 * (q % 2))
+        tcoef[q, 1] = box_rows(hk[q])
     arrive(c_copies)
     boxed = []
     for q in range(3):
-        tcoef[q] = box_rows(cext[q])
+        tcoef[q, 0] = box_rows(cext[q])
     for q in range(3):
-        boxed.append(box_y(tcoef.at[q]))
+        both = [box_y(tcoef.at[q, half]).reshape(64, 128) for half in range(2)]
+        boxed.append(dot(jnp.concatenate(both, axis=1), band).reshape(8, 8, 128))
     grad = -(fixed_ref[...] * boxed[0] + 2.0 * jext[0, pl.ds(4, 8), pl.ds(8, 8), :] * boxed[1] + boxed[2])
     for k in range(3):
         t = grad * slopes[k]
@@ -340,18 +344,17 @@
     group = as_float((iota((128, 128), 0) >> 2) == (iota((128, 128), 1) >> 2))
     s = smooth[...]
     u = dot(gsrc[...], group) * s * (1.0 - s)
-    cup[1] = u
-    z_g = along(cup.at[1], zg)
+    gslot[4] = u
+    edge_g[...] = pack([u[:8], u[8:]])
+    z_g = along(edge_g, zg_)
+    g_slots = slots(gslot)
     s_y = line("gy", na + nx, line_sum("gx", na, s_x))
-    arrive(z_g)
-    uh = halo(zg, lane2)
-    gslot[4] = 0.25 * (shifted(u, uh, -4, lane2) + 2.0 * u + shifted(u, uh, 4, lane2))
-    g_slots = slots(gslot)
     total = line_sum("gy", na + nx, s_y)
     sim_ref[...] = (jnp.sum(total) / count).reshape(1, 1)
     arrive(g_slots)
+    arrive(z_g)
     pick = as_float(iota((128, 32), 0) == (iota((128, 32), 1) << 2))
-    final = dot(dot(filt, gslot[...].reshape(144, 128)), pick)
+    final = dot(dot(filt, smooth_z(gslot, merged((zg_, None)))), pick)
     for k in range(3):
         for cx in range(2):
             out_ref[k, cx] = final[4 * k + 2 * cx:4 * k + 2 * cx + 2]
@@ -369,21 +372,24 @@
         count = float(fixed.size * nx * ny * na)
         f32 = jnp.float32
         vm = pltpu.VMEM
-        copies = 160 + nx + ny + na
+        copies = 192 + nx + ny + na
         sim, out = pl.pallas_call(
             functools.partial(kernel, (nx, ny, na), count),
             out_shape=(jax.ShapeDtypeStruct((1, 1), f32), jax.ShapeDtypeStruct(disp.shape, f32)),
-            in_specs=[pl.BlockSpec(memory_space=pltpu.VMEM)] * 4,
+            in_specs=[pl.BlockSpec(memory_space=pltpu.HBM)] * 4,
             out_specs=(pl.BlockSpec(memory_space=pltpu.VMEM),) * 2,
             scratch_shapes=[
-                vm((2, 16, 32), f32), vm((2, 16, 128), f32), vm((9, 16, 128), f32), vm((9, 16, 128), f32),
-                vm((16, 128), f32), vm((2, 16, 128), f32), vm((2, 16, 128), f32),
-                vm((4, 8, 128), f32), vm((4, 2, 8, 128), f32), vm((9, 8, 128), f32), vm((9, 8, 128), f32),
-                vm((12, 24, 128), f32), vm((16, 24, 128), f32), vm((16, 24, 128), f32), vm((8, 8, 128), f32),
+                vm(fixed.shape, f32), vm(moving.shape, f32), vm(disp.shape, f32), vm(offs.shape, jnp.int32),
+                pltpu.SemaphoreType.DMA((4,)),
+                vm((2, 16, 32), f32), vm((9, 16, 128), f32), vm((9, 16, 128), f32), vm((16, 128), f32),
+                vm((2, 8, 128), f32), vm((8, 128), f32), vm((2, 8, 128), f32), vm((8, 128), f32),
+                vm((2, 9, 2, 8, 128), f32), vm((2, 9, 8, 128), f32), vm((2, 9, 2, 8, 128), f32),
+                vm((2, 9, 8, 128), f32),
+                vm((12, 24, 128), f32), vm((16, 24, 128), f32), vm((16, 24, 128), f32), vm((3, 16, 24, 128), f32),
                 vm((1, 12, 24, 128), f32), vm((1, 16, 24, 128), f32), vm((1, 16, 24, 128), f32),
-                vm((3, 16, 24, 128), f32), vm((3, 8, 8, 128), f32), vm((5, 12, 24, 128), f32),
+                vm((3, 16, 24, 128), f32), vm((5, 12, 24, 128), f32),
                 vm((3, 8, 8, 128), f32), vm((16, 128), f32), vm((16, 128), f32),
-                vm((5, 2, 8, 24, 128), f32), vm((3, 8, 24, 128), f32), vm((nx + ny + na, 8, 128), f32),
+                vm((5, 2, 8, 24, 128), f32), vm((3, 2, 8, 24, 128), f32), vm((nx + ny + na, 8, 128), f32),
                 pltpu.SemaphoreType.DMA((copies,)), pltpu.SemaphoreType.DMA((copies,)),
             ],
             compiler_params=pltpu.CompilerParams(

time: 39 us -> 36 us (0.923)
  Pallas kernels: 32.8 us -> 29.7 us
    pallas_call x1, Pallas kernels: 32.8 us -> 29.7 us  [on_device(): pl.pallas_call(functools.partial(kernel, (nx, ny, na), count), out_shape=...]
where the time goes in v3:
time: 36 us; the launch traced here: 35.6 us
  Pallas kernels  29.7 us (82%)
  local copies, waits for them, and re-layouts  3.49 us (10%)
  between operations  2.4 us (7%)
    pallas_call x1, Pallas kernels, on_device(): pl.pallas_call(functools.partial(kernel, (nx, ny, na), count), out_shape=...  29.7 us
    unnamed x9, local copies, waits for them, and re-layouts  3.49 us

profile of v3, /device:TPU:0, one launch (start us, length us, event | category | flops | bytes accessed | tf_op | source)
XLA Modules:
  0.0 35.6 jit_solution(71003368346574425)
XLA Ops:
  0.6 0.0 copy-start
  0.6 0.7 %copy-done = f32[8,8,128]{2,1,0:T(8,128)S(1)} copy-done((f32[8,8,128]{2,1,0:T(8,128)S(1)}, f32[8,8,128]{2,1,0:T(8,128)}, u32[]{:S(2)}) %copy-start) | copy-done | bytes 32792
  1.4 0.0 copy-start.1
  1.4 0.8 %copy-done.1 = f32[8,8,128]{2,1,0:T(8,128)S(1)} copy-done((f32[8,8,128]{2,1,0:T(8,128)S(1)}, f32[8,8,128]{2,1,0:T(8,128)}, u32[]{:S(2)}) %copy-start.1) | copy-done | bytes 32792
  2.1 0.0 copy-start.2
  2.1 0.7 %copy-done.2 = f32[3,2,2,32]{3,2,1,0:T(2,128)S(1)} copy-done((f32[3,2,2,32]{3,2,1,0:T(2,128)S(1)}, f32[3,2,2,32]{3,2,1,0:T(2,128)}, u32[]{:S(2)}) %copy-start.2) | copy-done | bytes 1560
  2.8 0.0 copy-start.3
  2.8 0.7 %copy-done.3 = s32[3,2,2,32]{3,2,1,0:T(2,128)S(1)} copy-done((s32[3,2,2,32]{3,2,1,0:T(2,128)S(1)}, s32[3,2,2,32]{3,2,1,0:T(2,128)}, u32[]{:S(2)}) %copy-start.3) | copy-done | bytes 1560
  3.5 29.7 %shard_map.59 = (f32[1,1]{1,0:T(1,128)}, f32[3,2,2,32]{3,2,1,0:T(2,128)S(1)}) custom-call(f32[8,8,128]{2,1,0:T(8,128)S(1)} %copy-done, f32[8,8,128]{2,1,0:T(8,128)S(1)} %copy-done.1, f32[3,2,2,32]{3,2,1,0:T(2,128)S(1)} %copy-done.2, s32[3,2,2,32]{3,2,1,0:T(2,128)S(1)} %copy-done.3), custom_call_target="tpu_custom_call" | custom-call | tf_op jit(solution)/shard_map/pallas_call | solution.py:376
  33.9 0.6 %copy.9 = f32[3,2,2,32]{3,2,1,0:T(2,128)} copy(f32[3,2,2,32]{3,2,1,0:T(2,128)S(1)} %get-tuple-element.9) | data formatting | bytes 3072
Async XLA Ops:
  0.6 0.8 %copy-start = (f32[8,8,128]{2,1,0:T(8,128)S(1)}, f32[8,8,128]{2,1,0:T(8,128)}, u32[]{:S(2)}) copy-start(f32[8,8,128]{2,1,0:T(8,128)} %fixed_any.1) | copy-start | bytes 98308
  1.4 0.8 %copy-start.1 = (f32[8,8,128]{2,1,0:T(8,128)S(1)}, f32[8,8,128]{2,1,0:T(8,128)}, u32[]{:S(2)}) copy-start(f32[8,8,128]{2,1,0:T(8,128)} %moving_any.1) | copy-start | bytes 98308
  2.1 0.7 %copy-start.2 = (f32[3,2,2,32]{3,2,1,0:T(2,128)S(1)}, f32[3,2,2,32]{3,2,1,0:T(2,128)}, u32[]{:S(2)}) copy-start(f32[3,2,2,32]{3,2,1,0:T(2,128)} %disp_any.1) | copy-start | bytes 4612
  2.8 0.7 %copy-start.3 = (s32[3,2,2,32]{3,2,1,0:T(2,128)S(1)}, s32[3,2,2,32]{3,2,1,0:T(2,128)}, u32[]{:S(2)}) copy-start(s32[3,2,2,32]{3,2,1,0:T(2,128)} %offs_any.1) | copy-start | bytes 4612

commit v4 on v3

--- a/solution.py
+++ b/solution.py
@@ -67,11 +67,18 @@
     size = {"gx": nx, "gy": ny, "ga": na}
     pending = []
     counter = [0]
+    known = {}
 
     def target(**moves):
         return {a: me[a] + moves.get(a, 0) for a in me}
 
     def exists(moves):
+        key = tuple(moves.get(a, 0) for a in me)
+        if key not in known:
+            known[key] = inside(moves)
+        return known[key]
+
+    def inside(moves):
         conds = [((me[a] + d) >= 0) & ((me[a] + d) < size[a]) for a, d in moves.items() if d]
         return functools.reduce(jnp.logical_and, conds)
 
@@ -83,7 +90,7 @@
         to = exists(moves)
         origin = exists({a: -d for a, d in moves.items()})
         pl.when(to)(c.start)
-        pending.append((c, to))
+        pending.append((c, tuple(moves.get(a, 0) for a in me)))
         return c, origin
 
     def arrive(copies):
@@ -316,10 +323,9 @@
     edge_k[0] = pack(rows)
     edge_k[1] = pack([cc[i] for i in range(8)])
     z_k = along(edge_k, zk_)
-    c_copies = []
     for q, v in enumerate((ca, cb, cc)):
         cext[q, pl.ds(4, 8), pl.ds(8, 8), :] = v
-        c_copies += across(cext, q, 4)
+    c_copies = across(cext, pl.ds(0, 3), 4)
     s_a = line("ga", 0, jnp.sum(similar, axis=0))
     s_x = line("gx", na, line_sum("ga", 0, s_a))
     arrive(z_k)
@@ -358,11 +364,19 @@
     for k in range(3):
         for cx in range(2):
             out_ref[k, cx] = final[4 * k + 2 * cx:4 * k + 2 * cx + 2]
-    for c, to in pending:
-        if to is None:
-            c.wait_send()
+    groups = {}
+    for c, key in pending:
+        groups.setdefault(key, []).append(c)
+    for key, group in groups.items():
+
+        def finish(group=group):
+            for c in group:
+                c.wait_send()
+
+        if key is None:
+            finish()
         else:
-            pl.when(to)(c.wait_send)
+            pl.when(known[key])(finish)
 
 
 def solution(mesh):

time: 36 us -> 36 us (level)
  no operation moved by 1% of the time
where the time goes in v4:
time: 36 us; the launch traced here: 35.7 us
  Pallas kernels  29.8 us (83%)
  local copies, waits for them, and re-layouts  3.49 us (10%)
  between operations  2.4 us (7%)
    pallas_call x1, Pallas kernels, on_device(): pl.pallas_call(functools.partial(kernel, (nx, ny, na), count), out_shape=...  29.8 us
    unnamed x9, local copies, waits for them, and re-layouts  3.49 us

profile of v4, /device:TPU:0, one launch (start us, length us, event | category | flops | bytes accessed | tf_op | source)
XLA Modules:
  0.0 35.7 jit_solution(4286783392293406103)
XLA Ops:
  0.6 0.0 copy-start
  0.6 0.7 %copy-done = f32[8,8,128]{2,1,0:T(8,128)S(1)} copy-done((f32[8,8,128]{2,1,0:T(8,128)S(1)}, f32[8,8,128]{2,1,0:T(8,128)}, u32[]{:S(2)}) %copy-start) | copy-done | bytes 32792
  1.4 0.0 copy-start.1
  1.4 0.8 %copy-done.1 = f32[8,8,128]{2,1,0:T(8,128)S(1)} copy-done((f32[8,8,128]{2,1,0:T(8,128)S(1)}, f32[8,8,128]{2,1,0:T(8,128)}, u32[]{:S(2)}) %copy-start.1) | copy-done | bytes 32792
  2.1 0.0 copy-start.2
  2.1 0.7 %copy-done.2 = f32[3,2,2,32]{3,2,1,0:T(2,128)S(1)} copy-done((f32[3,2,2,32]{3,2,1,0:T(2,128)S(1)}, f32[3,2,2,32]{3,2,1,0:T(2,128)}, u32[]{:S(2)}) %copy-start.2) | copy-done | bytes 1560
  2.8 0.0 copy-start.3
  2.8 0.7 %copy-done.3 = s32[3,2,2,32]{3,2,1,0:T(2,128)S(1)} copy-done((s32[3,2,2,32]{3,2,1,0:T(2,128)S(1)}, s32[3,2,2,32]{3,2,1,0:T(2,128)}, u32[]{:S(2)}) %copy-start.3) | copy-done | bytes 1560
  3.5 29.8 %shard_map.59 = (f32[1,1]{1,0:T(1,128)}, f32[3,2,2,32]{3,2,1,0:T(2,128)S(1)}) custom-call(f32[8,8,128]{2,1,0:T(8,128)S(1)} %copy-done, f32[8,8,128]{2,1,0:T(8,128)S(1)} %copy-done.1, f32[3,2,2,32]{3,2,1,0:T(2,128)S(1)} %copy-done.2, s32[3,2,2,32]{3,2,1,0:T(2,128)S(1)} %copy-done.3), custom_call_target="tpu_custom_call" | custom-call | tf_op jit(solution)/shard_map/pallas_call | solution.py:390
  33.9 0.6 %copy.9 = f32[3,2,2,32]{3,2,1,0:T(2,128)} copy(f32[3,2,2,32]{3,2,1,0:T(2,128)S(1)} %get-tuple-element.9) | data formatting | bytes 3072
Async XLA Ops:
  0.6 0.8 %copy-start = (f32[8,8,128]{2,1,0:T(8,128)S(1)}, f32[8,8,128]{2,1,0:T(8,128)}, u32[]{:S(2)}) copy-start(f32[8,8,128]{2,1,0:T(8,128)} %fixed_any.1) | copy-start | bytes 98308
  1.4 0.8 %copy-start.1 = (f32[8,8,128]{2,1,0:T(8,128)S(1)}, f32[8,8,128]{2,1,0:T(8,128)}, u32[]{:S(2)}) copy-start(f32[8,8,128]{2,1,0:T(8,128)} %moving_any.1) | copy-start | bytes 98308
  2.1 0.7 %copy-start.2 = (f32[3,2,2,32]{3,2,1,0:T(2,128)S(1)}, f32[3,2,2,32]{3,2,1,0:T(2,128)}, u32[]{:S(2)}) copy-start(f32[3,2,2,32]{3,2,1,0:T(2,128)} %disp_any.1) | copy-start | bytes 4612
  2.8 0.7 %copy-start.3 = (s32[3,2,2,32]{3,2,1,0:T(2,128)S(1)}, s32[3,2,2,32]{3,2,1,0:T(2,128)}, u32[]{:S(2)}) copy-start(s32[3,2,2,32]{3,2,1,0:T(2,128)} %offs_any.1) | copy-start | bytes 4612
